TPU v7x, 32 devices: a whole 2x2x4 slice. The times are simulated.
32 devices in a mesh: dp: 16 (over z, y, core), blk: 2 (over x).
Axes of the slice: x: 2, y: 2, z: 4, core: 2. Of those that a mesh axis runs over, the one named last changes fastest.
Arguments:
- chars: int32 [2048, 16], P('blk', 'dp'), may hold values from 0 to 26
- timesteps: int32 [16], P('dp'), may hold values from 0 to 999
- embed: bfloat16 [27, 512], replicated, may hold values from -6 to 6
- ln1_gain: bfloat16 [2, 512], replicated, may hold values from 0.25 to 1.75
- ln1_bias: bfloat16 [2, 512], replicated, may hold values from -3 to 3
- w_time: bfloat16 [2, 512, 512], replicated, may hold values from -0.25 to 0.25
- w_qkv: bfloat16 [2, 512, 1536], replicated, may hold values from -0.25 to 0.25
- w_out: bfloat16 [2, 512, 512], replicated, may hold values from -6 to 6
- ln2_gain: bfloat16 [2, 512], replicated, may hold values from 0.25 to 1.75
- ln2_bias: bfloat16 [2, 512], replicated, may hold values from -3 to 3
- expand_weight: bfloat16 [2, 512, 2048], replicated, may hold values from -0.25 to 0.25
- expand_bias: bfloat16 [2, 2048], replicated, may hold values from -3 to 3
- contract_weight: bfloat16 [2, 2048, 512], replicated, may hold values from -0.125 to 0.125
- cotangent: bfloat16 [2048, 16, 512], P('blk', 'dp'), may hold values from -6 to 6
Outputs:
- activations: bfloat16 [2048, 16, 512], P('blk', 'dp')
- embed_grad: float32 [27, 512], replicated
- ln1_gain_grad: float32 [2, 512], replicated
- ln1_bias_grad: float32 [2, 512], replicated
- time_grad: float32 [2, 512, 512], replicated
- qkv_grad: float32 [2, 512, 1536], replicated
- out_grad: float32 [2, 512, 512], replicated
- ln2_gain_grad: float32 [2, 512], replicated
- ln2_bias_grad: float32 [2, 512], replicated
- up_grad: float32 [2, 512, 2048], replicated
- up_bias_grad: float32 [2, 2048], replicated
- down_grad: float32 [2, 2048, 512], replicated
All inputs are finite; a program needn't handle non-finite values.
Results may differ from a plain program's by a relative error of at most 0.015.
Values may be sent and summed in bfloat16 or wider, within the bound.
No kernel may reach another device: no remote copies, remote signals or barrier semaphores. Data moves between devices by JAX's collectives and lax.ppermute only.
A program may use at most 512 MiB of HBM per device.

v0:
```python
import math
from types import SimpleNamespace

import jax
import jax.numpy as jnp
from jax import lax
from jax.experimental import pallas as pl
from jax.experimental.pallas import tpu as pltpu
from jax.sharding import PartitionSpec as P

HEADS = 8
HEAD = 64
ROWS = 28
GROUP = 4
GROWS = ROWS * GROUP
CHUNK = 16
NROWS = ROWS * CHUNK
NGROUPS = CHUNK // GROUP
KPAD = 128
SLOT = 32
PIECE = 512
HALF = NROWS // 2
MASKED = -1e30
BF = jnp.bfloat16
F32 = jnp.float32
I32 = jnp.int32
MIB = 2**20
DEPTH = 3


def nn(a, b):
    return lax.dot_general(a, b, (((1,), (0,)), ((), ())), preferred_element_type=F32)


def nt(a, b):
    return lax.dot_general(a, b, (((1,), (1,)), ((), ())), preferred_element_type=F32)


def tn(a, b):
    return lax.dot_general(a, b, (((0,), (0,)), ((), ())), preferred_element_type=F32)


def iota(shape, dim):
    return lax.broadcasted_iota(I32, shape, dim)


def hi_lo(values):
    high = values.astype(BF)
    return high, (values - high.astype(F32)).astype(BF)


def row_seq(index):
    return lax.shift_right_logical(index * (65536 // ROWS + 1), 16)


def local_sums(chars_ref, cot_ref, place_ref, time_ref, count_ref, sum_ref, *, shares):
    positions = chars_ref.shape[1]
    chars = chars_ref[...]
    placed = (chars + place_ref[0] * ROWS == iota((KPAD, positions), 0)).astype(F32)
    counts = nt(jnp.ones((8, positions), BF), placed.astype(BF))[0:1]
    stamp = jnp.full((1, KPAD), time_ref[0].astype(F32) * (1.0 / shares), F32)
    row = jnp.concatenate([counts, stamp], axis=1)
    for device in range(count_ref.shape[0]):
        count_ref[device] = row
    onehot = (chars == iota((SLOT, positions), 0)).astype(F32)
    sum_ref[...] = nn(onehot.astype(BF), cot_ref[...])


def spread_sums(*refs):
    total = refs[0][...]
    for ref in refs[1:-1]:
        total = total + ref[...]
    total = total.astype(BF)
    for device in range(refs[-1].shape[0]):
        refs[-1][device] = total


class Loads:
    def __init__(self, depth):
        self.depth, self.queue, self.done = depth, [], set()

    def add(self, key, source, target, sem):
        self.queue.append((key, pltpu.make_async_copy(source, target, sem)))

    def begin(self):
        for _, copy in self.queue[: self.depth]:
            copy.start()
        self.started = min(self.depth, len(self.queue))

    def need(self, *keys):
        for key in keys:
            while key not in self.done:
                first, copy = self.queue[len(self.done)]
                copy.wait()
                self.done.add(first)
                if self.started < len(self.queue):
                    self.queue[self.started][1].start()
                    self.started += 1


def normalise(values):
    mean = jnp.mean(values, axis=-1, keepdims=True)
    centered = values - mean
    rstd = lax.rsqrt(jnp.mean(centered * centered, axis=-1, keepdims=True) + 1e-05)
    return centered * rstd, rstd


def norm_back(grad_out, unit, rstd, gain):
    scaled = grad_out * gain
    return rstd * (
        scaled
        - jnp.mean(scaled, axis=-1, keepdims=True)
        - unit * jnp.mean(scaled * unit, axis=-1, keepdims=True)
    )


def gelu_and_slope(up):
    size = jnp.abs(up)
    bell = jnp.exp2((-0.5 / math.log(2.0)) * (up * up))
    shift = math.sqrt(2.0) / 0.3275911
    ratio = 1.0 / (shift + size)
    poly = 0.5 * shift**5 * 1.061405429
    for power, term in ((4, -1.453152027), (3, 1.421413741), (2, -0.284496736), (1, 0.254829592)):
        poly = poly * ratio + 0.5 * shift**power * term
    tail = (poly * ratio) * bell
    slope = tail - (size * bell) * (1.0 / math.sqrt(2 * math.pi))
    return jnp.maximum(up, 0.0) - size * tail, jnp.where(up > 0, 1.0 - slope, slope)


def row_choices():
    row = iota((NROWS, 1), 0)
    seq_of = row_seq(row)
    char_of = row - seq_of * ROWS
    pick_char = (char_of == iota((NROWS, SLOT), 1)).astype(F32).astype(BF)
    pick_seq = (seq_of == iota((NROWS, CHUNK), 1)).astype(F32).astype(BF)
    return seq_of, char_of, pick_char, pick_seq


def side_masks():
    left = (iota((GROWS, KPAD), 1) < HEAD).astype(F32)
    return left.astype(BF), (1.0 - left).astype(BF)


def blocks(qkv, masks, group, pair, part):
    lanes = part * (qkv.shape[1] // 3) + pair * KPAD
    both = qkv[group * GROWS : (group + 1) * GROWS, lanes : lanes + KPAD]
    return jnp.concatenate([both * masks[0], both * masks[1]], axis=0)


def wide(ref, layer):
    return ref[layer : layer + 1, :].astype(F32)


KEPT = ("unit1", "rstd1", "norm1", "qkv", "probs", "att", "unit2", "rstd2", "norm2", "hid", "slp")


def kept_shapes(width, inner):
    row = {"rstd1": (KPAD, F32), "rstd2": (KPAD, F32), "qkv": (3 * width, BF), "hid": (inner, BF), "slp": (inner, BF)}
    shapes = {name: ((NROWS, row.get(name, (width, BF))[0]), row.get(name, (width, BF))[1]) for name in KEPT}
    shapes["probs"] = ((NGROUPS, HEADS // 2, 2 * GROWS, GROWS), BF)
    return [shapes[name] for name in KEPT]


def halves(size=HALF):
    return [slice(start, start + size) for start in range(0, NROWS, size)]


def groups_of(span):
    return range(span.start // GROWS, span.stop // GROWS)


def forward_tasks(layer, small, weight, kept, source, xs, mid, bias, masks, need):
    width = xs.shape[1]
    inner = kept.hid.shape[1]
    pairs = width // KPAD

    def normed(span, values, unit_ref, rstd_ref, norm_ref, gain, shift):
        unit, rstd = normalise(values[span, :])
        unit_ref[span, :] = unit.astype(BF)
        rstd_ref[span, :] = jnp.broadcast_to(rstd, (rstd.shape[0], KPAD))
        norm_ref[span, :] = (unit * wide(gain, layer) + wide(shift, layer)).astype(BF)

    def ln1(span):
        normed(span, source, kept.unit1, kept.rstd1, kept.norm1, small.g1, small.b1)

    def qkv(span):
        need("q")
        for part in range(3):
            lanes = slice(part * width, (part + 1) * width)
            product = nn(kept.norm1[span, :], weight.q[:, lanes])
            kept.qkv[span, lanes] = (product * 0.125 if part == 0 else product).astype(BF)

    def attend(span):
        for group in groups_of(span):
            rows = slice(group * GROWS, (group + 1) * GROWS)
            lanes = [slice(pair * KPAD, (pair + 1) * KPAD) for pair in range(pairs)]
            scores = [
                nt(blocks(kept.qkv, masks, group, pair, 1), kept.qkv[rows, lanes[pair]]) for pair in range(pairs)
            ]
            for pair in range(pairs):
                for side in range(2):
                    keys = slice(side * GROWS, (side + 1) * GROWS)
                    score = scores[pair][keys] + bias[group]
                    heft = jnp.exp(score - jnp.max(score, axis=0, keepdims=True))
                    prob = heft * (1.0 / jnp.sum(heft, axis=0, keepdims=True))
                    kept.probs[group, pair, keys, :] = prob.astype(BF)
            for pair in range(pairs):
                kept.att[rows, lanes[pair]] = tn(
                    kept.probs[group, pair], blocks(kept.qkv, masks, group, pair, 2)
                ).astype(BF)

    def out(span):
        need("o")
        mid[span, :] = source[span, :] + nn(kept.att[span, :], weight.o[...])

    def ln2(span):
        normed(span, mid, kept.unit2, kept.rstd2, kept.norm2, small.g2, small.b2)

    def up(span):
        need("e")
        for piece in range(inner // PIECE):
            cols = slice(piece * PIECE, (piece + 1) * PIECE)
            product = nn(kept.norm2[span, :], weight.e[:, cols])
            hidden, slope = gelu_and_slope(product + small.eb[layer : layer + 1, cols].astype(F32))
            kept.hid[span, cols] = hidden.astype(BF)
            kept.slp[span, cols] = slope.astype(BF)

    def down(span):
        need("c")
        xs[span, :] = mid[span, :] + nn(kept.hid[span, :], weight.c[...])

    parts = dict(ln1=ln1, qkv=qkv, attend=attend, out=out, ln2=ln2, up=up, down=down)
    return {
        f"{name}{half}": (lambda part=part, span=span: part(span))
        for name, part in parts.items()
        for half, span in enumerate(halves())
    }


def backward_tasks(layer, small, weight, kept, work, masks, need, send, features, picks, grads):
    xs, mid, acc = work.xs, work.mid, work.acc
    width = xs.shape[1]
    inner = kept.hid.shape[1]
    pairs = width // KPAD
    left_lanes = iota((GROWS, KPAD), 1) < HEAD

    def add_rows(ref, span, value, cols=slice(None)):
        total = jnp.sum(value, axis=0, keepdims=True)
        ref[layer : layer + 1, cols] = total if span.start == 0 else ref[layer : layer + 1, cols] + total

    def grad_up(span):
        need("c", "slp")
        for piece in range(inner // PIECE):
            cols = slice(piece * PIECE, (piece + 1) * PIECE)
            value = nt(work.gff[span, :], weight.c[cols, :]) * kept.slp[span, cols].astype(F32)
            add_rows(grads.ub, span, value, cols)
            work.gu[span, cols] = value.astype(BF)

    def grad_norm2(span):
        need("e")
        acc[span, :] = nt(work.gu[span, :], weight.e[...])

    def ln2_back(span):
        need("unit2", "rstd2")
        unit, grad = kept.unit2[span, :].astype(F32), acc[span, :]
        add_rows(grads.g2, span, grad * unit)
        add_rows(grads.b2, span, grad)
        total = xs[span, :] + norm_back(grad, unit, kept.rstd2[span, 0:1], wide(small.g2, layer))
        mid[span, :] = total
        work.gb[span, :] = total.astype(BF)

    def grad_att(span):
        need("o")
        work.ga[span, :] = nt(work.gb[span, :], weight.o[...]).astype(BF)

    def attend_back(span):
        need("qkv", "probs")
        for group in groups_of(span):
            rows = slice(group * GROWS, (group + 1) * GROWS)
            lanes = [slice(pair * KPAD, (pair + 1) * KPAD) for pair in range(pairs)]
            grad_probs = [
                nt(blocks(kept.qkv, masks, group, pair, 2), work.ga[rows, lanes[pair]]) for pair in range(pairs)
            ]
            for pair in range(pairs):
                for side in range(2):
                    keys = slice(side * GROWS, (side + 1) * GROWS)
                    prob = kept.probs[group, pair, keys, :].astype(F32)
                    grad_prob = grad_probs[pair][keys]
                    delta = jnp.sum(prob * grad_prob, axis=0, keepdims=True)
                    work.gscore[pair, keys, :] = (prob * (grad_prob - delta)).astype(BF)
            for pair in range(pairs):
                grad_score = work.gscore[pair]
                work.gproj[rows, lanes[pair]] = (
                    tn(grad_score, blocks(kept.qkv, masks, group, pair, 1)) * 0.125
                ).astype(BF)
                grad_key = nn(grad_score, kept.qkv[rows, lanes[pair]])
                grad_value = nn(kept.probs[group, pair], work.ga[rows, lanes[pair]])
                for part, product in ((1, grad_key), (2, grad_value)):
                    joined = jnp.where(left_lanes, product[0:GROWS], product[GROWS : 2 * GROWS])
                    start = part * width + pair * KPAD
                    work.gproj[rows, start : start + KPAD] = joined.astype(BF)

    def grad_norm1(span):
        need("q")
        acc[span, :] = nt(work.gproj[span, :], weight.q[...])

    def ln1_back(span):
        need("unit1", "rstd1")
        unit, grad = kept.unit1[span, :].astype(F32), acc[span, :]
        add_rows(grads.g1, span, grad * unit)
        add_rows(grads.b1, span, grad)
        total = mid[span, :] + norm_back(grad, unit, kept.rstd1[span, 0:1], wide(small.g1, layer))
        xs[span, :] = total
        work.gff[span, :] = total.astype(BF)

    def down_term():
        need("hid")
        send("down", layer, lambda: tn(kept.hid[...], work.gff[...]))

    def up_term():
        need("norm2")
        send("up", layer, lambda: tn(kept.norm2[...], work.gu[...]))

    def out_term():
        need("att")
        send("out", layer, lambda: tn(kept.att[...], work.gb[...]))

    def qkv_term():
        need("norm1")
        send("qkv", layer, lambda: tn(kept.norm1[...], work.gproj[...]))

    def time_term():
        pick_char, pick_seq = picks
        by_seq = tn(pick_seq, work.gff[...]).astype(BF)
        send("time", layer, lambda: tn(features, by_seq))
        if layer == 0:
            grads.eg[...] = tn(pick_char, work.gff[...])[0 : grads.eg.shape[0]]

    by_half = dict(
        grad_up=grad_up, grad_norm2=grad_norm2, ln2_back=ln2_back, grad_att=grad_att,
        attend_back=attend_back, grad_norm1=grad_norm1, ln1_back=ln1_back,
    )
    tasks = {
        f"{name}{half}": (lambda part=part, span=span: part(span))
        for name, part in by_half.items()
        for half, span in enumerate(halves(NROWS))
    }
    tasks.update(down_term=down_term, up_term=up_term, out_term=out_term, qkv_term=qkv_term, time_term=time_term)
    return tasks


FORWARD_ORDER = (
    "ln10", "ln11", "qkv0", "qkv1", "attend0", "attend1", "out0", "out1", "ln20", "ln21", "up0", "up1",
    "down0", "down1",
)
BACKWARD_ORDER = (
    "down_term", "grad_up0", "up_term", "grad_norm20", "ln2_back0", "out_term", "grad_att0", "attend_back0", "qkv_term", "grad_norm10", "ln1_back0", "time_term",
)


SMALLS = ("g1", "b1", "g2", "b2", "eb")


def bring(sources, targets, sems):
    copies = [pltpu.make_async_copy(a, b, sems.at[i]) for i, (a, b) in enumerate(zip(sources, targets))]
    for copy in copies:
        copy.start()
    return copies


def run_tasks(order, tasks):
    for name in order:
        tasks[name]()


def time_shift(features, weight, pick_seq):
    return nn(jnp.concatenate([pick_seq, pick_seq], axis=1), jnp.concatenate(hi_lo(nn(features, weight)), axis=0))


def first_layer(
    counts_ref, embed_hbm, g1_hbm, b1_hbm, g2_hbm, b2_hbm, eb_hbm,
    wt_hbm, wq_hbm, wo_hbm, we_hbm, wc_hbm,
    feat_ref, bias, xs, *rest
):
    count = len(KEPT)
    kept_hbm, rest = rest[:count], rest[count:]
    weight = SimpleNamespace(**dict(zip("tqoec", rest[:5])))
    kept_refs, rest = rest[5 : 5 + count], rest[5 + count :]
    kept = SimpleNamespace(**dict(zip(KEPT, kept_refs)))
    embed_ref, *smalls = rest[:6]
    later = rest[6]
    mid, in_sem, out_sem, small_sem = rest[7:]
    width = xs.shape[1]
    vocab = embed_ref.shape[0]
    small = SimpleNamespace(**dict(zip(SMALLS, smalls)))
    brought = bring((embed_hbm, g1_hbm, b1_hbm, g2_hbm, b2_hbm, eb_hbm), (embed_ref, *smalls), small_sem)
    loads = Loads(2)
    for index, (name, source) in enumerate(zip("tqoec", (wt_hbm, wq_hbm, wo_hbm, we_hbm, wc_hbm))):
        loads.add(name, source.at[0], getattr(weight, name), in_sem.at[index])
    loads.add("later", wt_hbm.at[1], later, in_sem.at[5])
    loads.begin()
    pushed = []

    def push(*names):
        for name in names:
            index = KEPT.index(name)
            pushed.append(pltpu.make_async_copy(kept_refs[index], kept_hbm[index], out_sem.at[index]))
            pushed[-1].start()

    _, _, pick_char, pick_seq = row_choices()
    masks = side_masks()

    shares = counts_ref.shape[0] // CHUNK
    stamp = []
    for group in range(NGROUPS):
        total = jnp.zeros((1, KPAD), F32)
        for member in range(GROUP):
            value = jnp.zeros((1, 2 * KPAD), F32)
            for share in range(shares):
                value = value + counts_ref[(group * GROUP + member) * shares + share]
            total = total + value[:, 0:KPAD]
            stamp.append(value[:, KPAD:])
        same = row_seq(iota((GROWS, GROWS), 1)) == row_seq(iota((GROWS, GROWS), 0))
        counts = jnp.broadcast_to(total[:, 0:GROWS], (GROWS, GROWS)).T
        live = same & (counts > 0.5)
        bias[group] = jnp.where(live, jnp.log(jnp.maximum(counts, 1.0)), MASKED)
    times = jnp.concatenate(stamp, axis=0)
    half = width // 2
    cycles = [
        times * jnp.exp((iota((1, KPAD), 1) + start).astype(F32) * (-math.log(10000.0) / half))
        for start in range(0, half, KPAD)
    ]
    features = jnp.concatenate(
        [jnp.sin(phase) for phase in cycles] + [jnp.cos(phase) for phase in cycles], axis=1
    ).astype(BF)
    feat_ref[...] = features
    for copy in brought:
        copy.wait()
    loads.need("t")
    xs[...] = nn(pick_char[:, 0:vocab], embed_ref[...]) + time_shift(features, weight.t[...], pick_seq)
    tasks = forward_tasks(0, small, weight, kept, xs, xs, mid, bias, masks, loads.need)
    after = {"ln11": ("unit1", "rstd1", "norm1"), "qkv1": ("qkv",), "attend1": ("probs", "att"),
             "ln21": ("unit2", "rstd2", "norm2"), "up1": ("hid", "slp")}
    for name in FORWARD_ORDER:
        tasks[name]()
        push(*after.get(name, ()))
    loads.need("later")
    xs[...] = xs[...] + time_shift(features, later[...], pick_seq)
    for copy in pushed:
        copy.wait()


def other_layers(
    own_ref, feat_ref, bias, x_ref, chars_hbm, g1_hbm, b1_hbm, g2_hbm, b2_hbm, eb_hbm,
    table_hbm, wt_hbm, wq_hbm, wo_hbm, we_hbm, wc_hbm, *rest, scale
):
    count = len(KEPT)
    layers, width = g1_hbm.shape
    kept_hbm, rest = rest[:count], rest[count:]
    act_hbm, *little_hbm = rest[:7]
    outs = dict(zip(("time", "qkv", "out", "up", "down"), rest[7:12]))
    rest = rest[12:]
    weights, kept = [], []
    for layer in range(layers):
        weights.append(SimpleNamespace(**dict(zip("tqoec", rest[:5]))))
        kept.append(SimpleNamespace(**dict(zip(KEPT, rest[5 : 5 + count]))))
        rest = rest[5 + count :]
    names = ("xs", "mid", "acc", "ga", "gproj", "gscore", "gu", "gb", "gff", "end", "act", "table")
    work = SimpleNamespace(**dict(zip(names, rest)))
    rest = rest[len(names) :]
    stages = dict(zip(outs, rest[:5]))
    little, rest = rest[5:11], rest[11:]
    (chars_ref, *smalls), rest = rest[:6], rest[6:]
    in_sem, kept_sem, out_sem, end_sem, small_sem, little_sem = rest
    eg, g1g, b1g, g2g, b2g, ubg = little
    xs, mid = work.xs, work.mid
    small = SimpleNamespace(**dict(zip(SMALLS, smalls)))
    brought = bring((chars_hbm, g1_hbm, b1_hbm, g2_hbm, b2_hbm, eb_hbm), (chars_ref, *smalls), small_sem)
    grads = SimpleNamespace(eg=eg, g1=g1g, b1=b1g, g2=g2g, b2=b2g, ub=ubg)
    sources = dict(zip("tqoec", (wt_hbm, wq_hbm, wo_hbm, we_hbm, wc_hbm)))
    loads = Loads(DEPTH)
    for layer in range(1, layers):
        for index, name in enumerate("tqoec"):
            if layer == 1 and name == "t":
                continue
            loads.add((layer, name), sources[name].at[layer], getattr(weights[layer], name), in_sem.at[index, layer])
    for name in ("slp", "c", "hid", "e", "norm2", "unit2", "rstd2", "o", "att", "probs", "qkv", "q", "norm1", "unit1", "rstd1"):
        if name in KEPT:
            index = KEPT.index(name)
            loads.add((0, name), kept_hbm[index], getattr(kept[0], name), kept_sem.at[index])
        else:
            loads.add((0, name), sources[name].at[0], getattr(weights[0], name), in_sem.at["tqoec".index(name), 0])
    loads.begin()
    table_copy = pltpu.make_async_copy(table_hbm, work.table, end_sem.at[2])
    table_copy.start()
    queued = {key for key, _ in loads.queue}

    def needs(layer):
        return lambda *names: loads.need(*((layer, name) for name in names if (layer, name) in queued))

    seq_of, char_of, pick_char, pick_seq = row_choices()
    masks = side_masks()
    features = feat_ref[...]
    for copy in brought:
        copy.wait()
    for layer in range(1, layers):
        source = x_ref if layer == 1 else xs
        if layer > 1:
            needs(layer)("t")
            xs[...] = xs[...] + time_shift(features, weights[layer].t[...], pick_seq)
        run_tasks(
            FORWARD_ORDER,
            forward_tasks(layer, small, weights[layer], kept[layer], source, xs, mid, bias, masks, needs(layer)),
        )

    own = own_ref[0]
    work.end[0:NROWS, :] = xs[...].astype(BF)
    work.end[NROWS:, :] = jnp.zeros((work.end.shape[0] - NROWS, width), BF)
    place = chars_ref[...] + lax.rem(own, GROUP) * ROWS
    hot = (place == iota((KPAD, chars_ref.shape[1]), 0)).astype(F32).astype(BF)
    start = pl.multiple_of(lax.div(own, GROUP) * GROWS, 16)
    work.act[...] = tn(hot, work.end[pl.ds(start, KPAD), :]).astype(BF)
    act_copy = pltpu.make_async_copy(work.act, act_hbm, end_sem.at[1])
    act_copy.start()

    slot_row = seq_of * SLOT + char_of
    spread = (slot_row == iota((NROWS, CHUNK * SLOT), 1)).astype(F32).astype(BF)
    table_copy.wait()
    incoming = nn(spread, work.table[...].reshape(CHUNK * SLOT, width)) * scale
    xs[...] = incoming
    work.gff[...] = incoming.astype(BF)

    sends = {}

    def send(name, layer, value):
        if name in sends:
            sends.pop(name).wait()
        stages[name][...] = value()
        copy = pltpu.make_async_copy(
            stages[name], outs[name].at[layer], out_sem.at[list(outs).index(name), layer]
        )
        copy.start()
        sends[name] = copy

    for layer in reversed(range(layers)):
        run_tasks(
            BACKWARD_ORDER,
            backward_tasks(layer, small, weights[layer], kept[layer], work, masks, needs(layer), send,
                           features, (pick_char, pick_seq), grads),
        )
    finals = bring(little, little_hbm, little_sem)
    act_copy.wait()
    for copy in [*sends.values(), *finals]:
        copy.wait()


def vmem():
    return pl.BlockSpec(memory_space=pltpu.VMEM)


def smem():
    return pl.BlockSpec(memory_space=pltpu.SMEM)


def anywhere():
    return pl.BlockSpec(memory_space=pl.ANY)


def call(body, outs, ins, in_specs, out_specs, scratch=(), name=None, mib=8):
    return pl.pallas_call(
        body,
        out_shape=outs,
        in_specs=in_specs,
        out_specs=out_specs,
        scratch_shapes=list(scratch),
        compiler_params=pltpu.CompilerParams(vmem_limit_bytes=mib * MIB),
        name=name,
    )(*ins)


def far(array):
    return pltpu.with_memory_space_constraint(array, pltpu.HBM)


def keep(array):
    return pltpu.with_memory_space_constraint(array, pltpu.VMEM)


def run_forward(counts, weights, big):
    (embed, ln1_gain, ln1_bias, _, _, _, ln2_gain, ln2_bias, _, expand_bias, _) = weights
    width, inner = embed.shape[1], expand_bias.shape[1]
    shapes = kept_shapes(width, inner)
    table = (NROWS, width)
    smalls = (embed, ln1_gain, ln1_bias, ln2_gain, ln2_bias, expand_bias)
    return call(
        first_layer,
        [
            pltpu.VMEM((CHUNK, width), BF),
            pltpu.VMEM((NGROUPS, GROWS, GROWS), F32),
            pltpu.VMEM(table, F32),
        ]
        + [pltpu.HBM(shape, dtype) for shape, dtype in shapes],
        (counts, *map(far, smalls), *map(far, big)),
        [vmem()] + [anywhere()] * (6 + len(big)),
        [vmem()] * 3 + [anywhere()] * len(shapes),
        [pltpu.VMEM(w.shape[1:], w.dtype) for w in big]
        + [pltpu.VMEM(shape, dtype) for shape, dtype in shapes]
        + [
            pltpu.VMEM(small.shape, BF) for small in smalls
        ]
        + [
            pltpu.VMEM(big[0].shape[1:], BF),
            pltpu.VMEM(table, F32),
            pltpu.SemaphoreType.DMA((len(big) + 1,)),
            pltpu.SemaphoreType.DMA((len(shapes),)),
            pltpu.SemaphoreType.DMA((len(smalls),)),
        ],
        name="forward",
        mib=40,
    )


def run_backward(own, chars_row, table, weights, big, passed, scale):
    (embed, ln1_gain, ln1_bias, w_time, w_qkv, w_out, ln2_gain, ln2_bias, expand_weight, expand_bias,
     contract_weight) = weights
    layers, width = ln1_gain.shape
    inner = expand_bias.shape[1]
    shapes = kept_shapes(width, inner)
    positions = chars_row.shape[1]
    whole = (NROWS, width)

    def f32_like(array):
        return jax.ShapeDtypeStruct(array.shape, F32)

    features, bias, x, *kept = passed
    layer_scratch = [pltpu.VMEM(w.shape[1:], w.dtype) for w in big] + [
        pltpu.VMEM(shape, dtype) for shape, dtype in shapes
    ]
    smalls = (ln1_gain, ln1_bias, ln2_gain, ln2_bias, expand_bias)
    little = (embed, *smalls)
    outs = call(
        lambda *refs: other_layers(*refs, scale=scale),
        [jax.ShapeDtypeStruct((positions, width), BF)]
        + [f32_like(w) for w in (*little, w_time, w_qkv, w_out, expand_weight, contract_weight)],
        (own, keep(features), keep(bias), keep(x), far(chars_row), *map(far, smalls), keep(table), *map(far, big),
         *map(far, kept)),
        [smem()] + [vmem()] * 3 + [anywhere()] * (7 + len(big) + len(kept)),
        [anywhere()] * 12,
        layer_scratch * layers
        + [
            pltpu.VMEM(whole, F32),
            pltpu.VMEM(whole, F32),
            pltpu.VMEM(whole, F32),
            pltpu.VMEM(whole, BF),
            pltpu.VMEM((NROWS, 3 * width), BF),
            pltpu.VMEM((HEADS // 2, 2 * GROWS, GROWS), BF),
            pltpu.VMEM((NROWS, inner), BF),
            pltpu.VMEM(whole, BF),
            pltpu.VMEM(whole, BF),
            pltpu.VMEM((NROWS + KPAD - GROWS, width), BF),
            pltpu.VMEM((positions, width), BF),
            pltpu.VMEM(table.shape, BF),
        ]
        + [pltpu.VMEM(w.shape[1:], F32) for w in big]
        + [pltpu.VMEM(w.shape, F32) for w in little]
        + [pltpu.VMEM(chars_row.shape, I32)]
        + [pltpu.VMEM(small.shape, BF) for small in smalls]
        + [
            pltpu.SemaphoreType.DMA((len(big), layers)),
            pltpu.SemaphoreType.DMA((len(shapes),)),
            pltpu.SemaphoreType.DMA((len(big), layers)),
            pltpu.SemaphoreType.DMA((3,)),
            pltpu.SemaphoreType.DMA((1 + len(smalls),)),
            pltpu.SemaphoreType.DMA((len(little),)),
        ],
        name="backward",
        mib=60,
    )
    act, eg, g1, b1, g2, b2, ub, tg, qg, og, ug, dg = outs
    return act, (eg, g1, b1, tg, qg, og, g2, b2, ug, ub, dg)


def per_device(chars, timesteps, *rest):
    weights, cotangent = rest[:-1], rest[-1]
    width = weights[0].shape[1]
    n_dp, n_blk = lax.axis_size("dp"), lax.axis_size("blk")
    seq = lax.axis_index("dp")
    positions = chars.shape[0]
    chars_row = chars.reshape(1, positions)
    big = [weights[i] for i in (3, 4, 5, 8, 10)]
    counts, sums = call(
        lambda *refs: local_sums(*refs, shares=n_blk),
        [
            jax.ShapeDtypeStruct((n_dp * n_blk, 1, 2 * KPAD), F32),
            jax.ShapeDtypeStruct((SLOT, width), F32),
        ],
        (
            far(chars_row),
            far(cotangent.reshape(positions, width)),
            (seq % GROUP).astype(I32).reshape(1),
            timesteps,
        ),
        [vmem(), vmem(), smem(), smem()],
        [vmem(), vmem()],
        name="local_sums",
    )
    counts = lax.all_to_all(counts, ("dp", "blk"), split_axis=0, concat_axis=0, tiled=True)
    parts = [sums] + [
        lax.ppermute(sums, "blk", [(i, (i + step) % n_blk) for i in range(n_blk)])
        for step in range(1, n_blk)
    ]
    table = call(
        spread_sums,
        jax.ShapeDtypeStruct((n_dp, SLOT, width), BF),
        parts,
        [vmem()] * len(parts),
        vmem(),
        name="spread_sums",
    )
    table = lax.all_to_all(table, "dp", split_axis=0, concat_axis=0, tiled=True)
    scale = 1.0 / (n_dp * n_blk)
    if n_dp == CHUNK:
        kept = run_forward(counts, weights, big)
        act, grads = run_backward(seq.reshape(1).astype(I32), chars_row, table, weights, big, kept, scale)
    else:

        def step(carry, chunk):
            act, grads = carry
            place = seq - chunk * CHUNK
            inside = (place >= 0) & (place < CHUNK)
            here = lax.dynamic_slice_in_dim(counts, chunk * CHUNK * n_blk, CHUNK * n_blk, axis=0)
            part = lax.dynamic_slice_in_dim(table, chunk * CHUNK, CHUNK, axis=0)
            own = jnp.clip(place, 0, CHUNK - 1).reshape(1).astype(I32)
            kept = run_forward(here, weights, big)
            new_act, new_grads = run_backward(own, chars_row, part, weights, big, kept, scale)
            return (jnp.where(inside, new_act, act), tuple(a + b for a, b in zip(grads, new_grads))), None

        start = (jnp.zeros((positions, width), BF), tuple(jnp.zeros(w.shape, F32) for w in weights))
        (act, grads), _ = lax.scan(step, start, jnp.arange(n_dp // CHUNK, dtype=I32))
    return (act.reshape(positions, 1, width), *grads)


def solution(mesh):
    in_specs = (P("blk", "dp"), P("dp")) + (P(),) * 11 + (P("blk", "dp", None),)
    out_specs = (P("blk", "dp", None),) + (P(),) * 11
    return jax.shard_map(
        per_device, mesh=mesh, in_specs=in_specs, out_specs=out_specs, check_vma=False
    )
```

profile of v0, /device:TPU:0, one launch (start us, length us, event | category | flops | bytes accessed | tf_op | source)
XLA Modules:
  0.0 69.7 jit_solution(5200926950483030494)
XLA Ops:
  1.3 2.1 %local_sums.1 = (f32[32,1,256]{2,1,0:T(1,128)}, f32[32,512]{1,0:T(8,128)S(1)}) custom-call(s32[1,1024]{1,0:T(1,128)} %bitcast.6, bf16[1024,512]{1,0:T(8,128)(2,1)} %bitcast.5, s32[1]{0:T(128)} %bitcast.3.refs_2_, s32[1]{0:T(128)S(6)} %copy.26.refs_3_), custom_call_target="tpu_custom_call" | custom-call | tf_op jit(solution)/shard_map/local_sums/pallas_call | solution.py:570
  3.4 2.9 %collective-permute-start = (f32[32,512]{1,0:T(8,128)S(1)}, f32[32,512]{1,0:T(8,128)S(1)}, u32[]{:S(2)}, u32[]{:S(2)}) collective-permute-start(f32[32,512]{1,0:T(8,128)S(1)} %get-tuple-element.44.refs_0_), channel_id=1, source_target_pairs={{0,1},{1,0},{2,3},{3,2},{4,5},{5,4},{6,7},{7,6},{8,9},{9,8},{10,11... | collective-permute-start | bytes 196616 | tf_op jit(solution)/shard_map/ppermute | solution.py:709
  6.3 4.9 %all-to-all-start = ((f32[32,1,256]{2,1,0:T(1,128)}), f32[32,1,256]{2,1,0:T(1,128)S(1)}, u32[]{:S(2)}, u32[]{:S(2)}) async-start(f32[32,1,256]{2,1,0:T(1,128)} %get-tuple-element.40), calls=%async_computation | async-start | bytes 65536 | tf_op jit(solution)/shard_map/all_to_all | solution.py:707
  11.3 0.0 collective-permute-done.refs_1_
  11.3 0.9 %spread_sums.1 = bf16[16,32,512]{2,1,0:T(8,128)(2,1)} custom-call(f32[32,512]{1,0:T(8,128)S(1)} %get-tuple-element.44.refs_0_, f32[32,512]{1,0:T(8,128)S(1)} %collective-permute-done.refs_1_), custom_call_target="tpu_custom_call" | custom-call | tf_op jit(solution)/shard_map/spread_sums/pallas_call | solution.py:570
  12.1 6.5 %all-to-all-done.counts_ref = f32[32,1,256]{2,1,0:T(1,128)S(1)} async-done(((f32[32,1,256]{2,1,0:T(1,128)}), f32[32,1,256]{2,1,0:T(1,128)S(1)}, u32[]{:S(2)}, u32[]{:S(2)}) %all-to-all-start) | async-done | bytes 32800 | tf_op jit(solution)/shard_map/all_to_all | solution.py:707
  18.6 3.6 %all-to-all-start.1 = ((bf16[16,32,512]{2,1,0:T(8,128)(2,1)}), bf16[16,32,512]{2,1,0:T(8,128)(2,1)S(1)}, u32[]{:S(2)}, u32[]{:S(2)}) async-start(bf16[16,32,512]{2,1,0:T(8,128)(2,1)} %spread_sums.1), calls=%async_computation.1 | async-start | bytes 1048576 | tf_op jit(solution)/shard_map/all_to_all | solution.py:720
  22.2 11.0 %forward.1 = (bf16[16,512]{1,0:T(8,128)(2,1)S(1)}, f32[4,112,112]{2,1,0:T(8,128)S(1)}, f32[448,512]{1,0:T(8,128)S(1)}, bf16[448,512]{1,0:T(8,128)(2,1)}, f32[448...) custom-call(f32[32,1,256]{2,1,0:T(1,128)S(1)} %all-to-all-done.count, ...), custom_call_target="tpu_custom_call" | custom-call | tf_op jit(solution)/shard_map/forward/pallas_call | solution.py:570
  33.2 3.5 %all-to-all-done.1.refs_10_ = bf16[16,32,512]{2,1,0:T(8,128)(2,1)S(1)} async-done(((bf16[16,32,512]{2,1,0:T(8,128)(2,1)}), bf16[16,32,512]{2,1,0:T(8,128)(2,1)S(1)}, u32[]{:S(2)}, u32[]{:S(2)}) %all-to-all-start.1) | async-done | bytes 524320 | tf_op jit(solution)/shard_map/all_to_all | solution.py:720
  36.6 32.9 %backward.1 = (bf16[1024,512]{1,0:T(8,128)(2,1)}, f32[27,512]{1,0:T(8,128)}, f32[2,512]{1,0:T(2,128)}, f32[2,512]{1,0:T(2,128)}, f32[2,512]{1,0:T(2,128)}, /*ind...) custom-call(s32[1]{0:T(128)} %bitcast.refs_0_, ...), custom_call_target="tpu_custom_call" | custom-call | tf_op jit(solution)/shard_map/backward/pallas_call | solution.py:570
Async XLA Ops:
  3.4 7.9 %collective-permute-start = (f32[32,512]{1,0:T(8,128)S(1)}, f32[32,512]{1,0:T(8,128)S(1)}, u32[]{:S(2)}, u32[]{:S(2)}) collective-permute-start(f32[32,512]{1,0:T(8,128)S(1)} %get-tuple-element.44.refs_0_), channel_id=1, source_target_pairs={{0,1},{1,0},{2,3},{3,2},{4,5},{5,4},{6,7},{7,6},{8,9},{9,8},{10,11... | collective-permute-start | bytes 196616 | tf_op jit(solution)/shard_map/ppermute | solution.py:709
  6.3 12.3 %all-to-all-start = ((f32[32,1,256]{2,1,0:T(1,128)}), f32[32,1,256]{2,1,0:T(1,128)S(1)}, u32[]{:S(2)}, u32[]{:S(2)}) async-start(f32[32,1,256]{2,1,0:T(1,128)} %get-tuple-element.40), calls=%async_computation | async-start | bytes 65536 | tf_op jit(solution)/shard_map/all_to_all | solution.py:707
  18.6 18.0 %all-to-all-start.1 = ((bf16[16,32,512]{2,1,0:T(8,128)(2,1)}), bf16[16,32,512]{2,1,0:T(8,128)(2,1)S(1)}, u32[]{:S(2)}, u32[]{:S(2)}) async-start(bf16[16,32,512]{2,1,0:T(8,128)(2,1)} %spread_sums.1), calls=%async_computation.1 | async-start | bytes 1048576 | tf_op jit(solution)/shard_map/all_to_all | solution.py:720
where the time goes:
time: 70.1 us; the launch traced here: 69.7 us
  Pallas kernels  46.8 us (67%)
  starting transfers between devices  11.4 us (16%)
  waiting for transfers between devices  9.95 us (14%)
  between operations  1.52 us (2%)
    pallas_call x4, Pallas kernels, call(): pl.pallas_call(body, out_shape=outs, in_specs=in_specs, out_specs=out_spe...  46.8 us
    all_to_all x1, waiting for transfers between devices, per_device(): lax.all_to_all(counts, ('dp', 'blk'), split_axis=0, concat_axis=0, tiled=...  6.49 us
    all_to_all x1, starting transfers between devices, per_device(): lax.all_to_all(counts, ('dp', 'blk'), split_axis=0, concat_axis=0, tiled=...  4.92 us
    all_to_all x1, starting transfers between devices, per_device(): table = lax.all_to_all(table, 'dp', split_axis=0, concat_axis=0, tiled=True)  3.57 us
    all_to_all x1, waiting for transfers between devices, per_device(): table = lax.all_to_all(table, 'dp', split_axis=0, concat_axis=0, tiled=True)  3.46 us
    ppermute x1, starting transfers between devices, per_device(): lax.ppermute(sums, 'blk', [(i, (i + step) % n_blk) for i in range(n_blk)])  2.94 us
  transfers between devices with their start and end apart: 3, of which 2 were waited for; matrix products, arithmetic and copies ran while one was open for 0% of the time, Pallas kernels for 17%

commit v1 on v0

--- a/solution.py
+++ b/solution.py
@@ -25,7 +25,12 @@
 F32 = jnp.float32
 I32 = jnp.int32
 MIB = 2**20
-DEPTH = 3
+DEPTH = 2
+GSTRIP = 112
+NSTRIP = 112
+WIDE = 256
+BAND = 512
+PER_TASK = 1
 
 
 def nn(a, b):
@@ -83,19 +88,22 @@
         self.queue.append((key, pltpu.make_async_copy(source, target, sem)))
 
     def begin(self):
-        for _, copy in self.queue[: self.depth]:
-            copy.start()
-        self.started = min(self.depth, len(self.queue))
+        self.started = 0
+        self.advance(self.depth)
 
     def need(self, *keys):
         for key in keys:
             while key not in self.done:
+                if len(self.done) == self.started:
+                    self.advance(1)
                 first, copy = self.queue[len(self.done)]
                 copy.wait()
                 self.done.add(first)
-                if self.started < len(self.queue):
-                    self.queue[self.started][1].start()
-                    self.started += 1
+
+    def advance(self, count):
+        for _, copy in self.queue[self.started : self.started + count]:
+            copy.start()
+        self.started = min(self.started + count, len(self.queue))
 
 
 def normalise(values):
@@ -151,6 +159,7 @@
     return ref[layer : layer + 1, :].astype(F32)
 
 
+EARLY = ("unit1", "rstd1", "norm1", "qkv", "probs")
 KEPT = ("unit1", "rstd1", "norm1", "qkv", "probs", "att", "unit2", "rstd2", "norm2", "hid", "slp")
 
 
@@ -165,17 +174,23 @@
     return [slice(start, start + size) for start in range(0, NROWS, size)]
 
 
+def strips(span, rows):
+    return [slice(start, start + rows) for start in range(span.start, span.stop, rows)]
+
+
 def groups_of(span):
     return range(span.start // GROWS, span.stop // GROWS)
 
 
-def forward_tasks(layer, small, weight, kept, source, xs, mid, bias, masks, need):
+def forward_tasks(layer, small, weight, kept, source, xs, mid, bias, masks, need, brought, shifted=None):
     width = xs.shape[1]
     inner = kept.hid.shape[1]
     pairs = width // KPAD
 
     def normed(span, values, unit_ref, rstd_ref, norm_ref, gain, shift):
         unit, rstd = normalise(values[span, :])
+        while brought:
+            brought.pop().wait()
         unit_ref[span, :] = unit.astype(BF)
         rstd_ref[span, :] = jnp.broadcast_to(rstd, (rstd.shape[0], KPAD))
         norm_ref[span, :] = (unit * wide(gain, layer) + wide(shift, layer)).astype(BF)
@@ -197,6 +212,7 @@
             scores = [
                 nt(blocks(kept.qkv, masks, group, pair, 1), kept.qkv[rows, lanes[pair]]) for pair in range(pairs)
             ]
+            yield
             for pair in range(pairs):
                 for side in range(2):
                     keys = slice(side * GROWS, (side + 1) * GROWS)
@@ -204,10 +220,12 @@
                     heft = jnp.exp(score - jnp.max(score, axis=0, keepdims=True))
                     prob = heft * (1.0 / jnp.sum(heft, axis=0, keepdims=True))
                     kept.probs[group, pair, keys, :] = prob.astype(BF)
+            yield
             for pair in range(pairs):
                 kept.att[rows, lanes[pair]] = tn(
                     kept.probs[group, pair], blocks(kept.qkv, masks, group, pair, 2)
                 ).astype(BF)
+            yield
 
     def out(span):
         need("o")
@@ -221,13 +239,21 @@
         for piece in range(inner // PIECE):
             cols = slice(piece * PIECE, (piece + 1) * PIECE)
             product = nn(kept.norm2[span, :], weight.e[:, cols])
-            hidden, slope = gelu_and_slope(product + small.eb[layer : layer + 1, cols].astype(F32))
-            kept.hid[span, cols] = hidden.astype(BF)
-            kept.slp[span, cols] = slope.astype(BF)
+            shift = small.eb[layer : layer + 1, cols].astype(F32)
+            for rows in strips(span, GSTRIP):
+                strip = product[rows.start - span.start : rows.stop - span.start]
+                hidden, slope = gelu_and_slope(strip + shift)
+                kept.hid[rows, cols] = hidden.astype(BF)
+                kept.slp[rows, cols] = slope.astype(BF)
+                yield
 
     def down(span):
         need("c")
-        xs[span, :] = mid[span, :] + nn(kept.hid[span, :], weight.c[...])
+        for start in range(0, width, WIDE):
+            cols = slice(start, start + WIDE)
+            total = mid[span, cols] + nn(kept.hid[span, :], weight.c[:, cols])
+            xs[span, cols] = total if shifted is None else total + shifted[span, cols]
+            yield
 
     parts = dict(ln1=ln1, qkv=qkv, attend=attend, out=out, ln2=ln2, up=up, down=down)
     return {
@@ -262,12 +288,14 @@
 
     def ln2_back(span):
         need("unit2", "rstd2")
-        unit, grad = kept.unit2[span, :].astype(F32), acc[span, :]
-        add_rows(grads.g2, span, grad * unit)
-        add_rows(grads.b2, span, grad)
-        total = xs[span, :] + norm_back(grad, unit, kept.rstd2[span, 0:1], wide(small.g2, layer))
-        mid[span, :] = total
-        work.gb[span, :] = total.astype(BF)
+        for rows in strips(span, NSTRIP):
+            unit, grad = kept.unit2[rows, :].astype(F32), acc[rows, :]
+            add_rows(grads.g2, rows, grad * unit)
+            add_rows(grads.b2, rows, grad)
+            total = xs[rows, :] + norm_back(grad, unit, kept.rstd2[rows, 0:1], wide(small.g2, layer))
+            mid[rows, :] = total
+            work.gb[rows, :] = total.astype(BF)
+            yield
 
     def grad_att(span):
         need("o")
@@ -281,6 +309,7 @@
             grad_probs = [
                 nt(blocks(kept.qkv, masks, group, pair, 2), work.ga[rows, lanes[pair]]) for pair in range(pairs)
             ]
+            yield
             for pair in range(pairs):
                 for side in range(2):
                     keys = slice(side * GROWS, (side + 1) * GROWS)
@@ -288,6 +317,7 @@
                     grad_prob = grad_probs[pair][keys]
                     delta = jnp.sum(prob * grad_prob, axis=0, keepdims=True)
                     work.gscore[pair, keys, :] = (prob * (grad_prob - delta)).astype(BF)
+            yield
             for pair in range(pairs):
                 grad_score = work.gscore[pair]
                 work.gproj[rows, lanes[pair]] = (
@@ -299,6 +329,7 @@
                     joined = jnp.where(left_lanes, product[0:GROWS], product[GROWS : 2 * GROWS])
                     start = part * width + pair * KPAD
                     work.gproj[rows, start : start + KPAD] = joined.astype(BF)
+            yield
 
     def grad_norm1(span):
         need("q")
@@ -306,33 +337,35 @@
 
     def ln1_back(span):
         need("unit1", "rstd1")
-        unit, grad = kept.unit1[span, :].astype(F32), acc[span, :]
-        add_rows(grads.g1, span, grad * unit)
-        add_rows(grads.b1, span, grad)
-        total = mid[span, :] + norm_back(grad, unit, kept.rstd1[span, 0:1], wide(small.g1, layer))
-        xs[span, :] = total
-        work.gff[span, :] = total.astype(BF)
+        for rows in strips(span, NSTRIP):
+            unit, grad = kept.unit1[rows, :].astype(F32), acc[rows, :]
+            add_rows(grads.g1, rows, grad * unit)
+            add_rows(grads.b1, rows, grad)
+            total = mid[rows, :] + norm_back(grad, unit, kept.rstd1[rows, 0:1], wide(small.g1, layer))
+            xs[rows, :] = total
+            work.gff[rows, :] = total.astype(BF)
+            yield
 
     def down_term():
         need("hid")
-        send("down", layer, lambda: tn(kept.hid[...], work.gff[...]))
+        yield from send("down", layer, kept.hid, work.gff)
 
     def up_term():
         need("norm2")
-        send("up", layer, lambda: tn(kept.norm2[...], work.gu[...]))
+        yield from send("up", layer, kept.norm2, work.gu)
 
     def out_term():
         need("att")
-        send("out", layer, lambda: tn(kept.att[...], work.gb[...]))
+        yield from send("out", layer, kept.att, work.gb)
 
     def qkv_term():
         need("norm1")
-        send("qkv", layer, lambda: tn(kept.norm1[...], work.gproj[...]))
+        yield from send("qkv", layer, kept.norm1, work.gproj)
 
     def time_term():
         pick_char, pick_seq = picks
         by_seq = tn(pick_seq, work.gff[...]).astype(BF)
-        send("time", layer, lambda: tn(features, by_seq))
+        yield from send("time", layer, features, by_seq)
         if layer == 0:
             grads.eg[...] = tn(pick_char, work.gff[...])[0 : grads.eg.shape[0]]
 
@@ -349,9 +382,14 @@
     return tasks
 
 
+FIRST_ORDER = (
+    "ln10", "ln11", "qkv0", "qkv1", "attend0", "attend1", "out0", "out1", "shift0", "ln20", "ln21", "up0", "up1",
+    "down0", "down1",
+)
+SECOND_ORDER = ("ln10", "ln11", "qkv0", "qkv1", "attend0", "attend1")
+LATTER_ORDER = ("out0", "out1", "ln20", "ln21", "up0", "down0|up1", "down1")
 FORWARD_ORDER = (
-    "ln10", "ln11", "qkv0", "qkv1", "attend0", "attend1", "out0", "out1", "ln20", "ln21", "up0", "up1",
-    "down0", "down1",
+    "ln10", "ln11", "qkv0", "qkv1", "attend0", "out0", "ln20", "attend1|up0", "out1", "ln21", "down0|up1", "down1",
 )
 BACKWARD_ORDER = (
     "down_term", "grad_up0", "up_term", "grad_norm20", "ln2_back0", "out_term", "grad_att0", "attend_back0", "qkv_term", "grad_norm10", "ln1_back0", "time_term",
@@ -368,9 +406,16 @@
     return copies
 
 
-def run_tasks(order, tasks):
-    for name in order:
-        tasks[name]()
+def run_parts(names, tasks):
+    steps = [step for step in (tasks[name]() for name in names.split("|")) if step is not None]
+    while steps:
+        steps = [step for step in steps if next(step, steps) is not steps]
+
+
+def run_tasks(order, tasks, loads):
+    for names in order:
+        run_parts(names, tasks)
+        loads.advance(PER_TASK)
 
 
 def time_shift(features, weight, pick_seq):
@@ -380,16 +425,17 @@
 def first_layer(
     counts_ref, embed_hbm, g1_hbm, b1_hbm, g2_hbm, b2_hbm, eb_hbm,
     wt_hbm, wq_hbm, wo_hbm, we_hbm, wc_hbm,
-    feat_ref, bias, xs, *rest
+    feat_ref, xs, next_att, next_o, *rest
 ):
     count = len(KEPT)
-    kept_hbm, rest = rest[:count], rest[count:]
+    kept_hbm, early_hbm, rest = rest[:count], rest[count : count + len(EARLY)], rest[count + len(EARLY) :]
     weight = SimpleNamespace(**dict(zip("tqoec", rest[:5])))
     kept_refs, rest = rest[5 : 5 + count], rest[5 + count :]
     kept = SimpleNamespace(**dict(zip(KEPT, kept_refs)))
+    early_refs, rest = rest[: len(EARLY)], rest[len(EARLY) :]
+    early = SimpleNamespace(att=next_att, hid=kept.hid, **dict(zip(EARLY, early_refs)))
     embed_ref, *smalls = rest[:6]
-    later = rest[6]
-    mid, in_sem, out_sem, small_sem = rest[7:]
+    later, next_q, bias, mid, shifted, in_sem, out_sem, early_sem, small_sem = rest[6:]
     width = xs.shape[1]
     vocab = embed_ref.shape[0]
     small = SimpleNamespace(**dict(zip(SMALLS, smalls)))
@@ -397,14 +443,21 @@
     loads = Loads(2)
     for index, (name, source) in enumerate(zip("tqoec", (wt_hbm, wq_hbm, wo_hbm, we_hbm, wc_hbm))):
         loads.add(name, source.at[0], getattr(weight, name), in_sem.at[index])
-    loads.add("later", wt_hbm.at[1], later, in_sem.at[5])
+        if name == "o":
+            loads.add("later", wt_hbm.at[1], later, in_sem.at[5])
+    loads.add("next_q", wq_hbm.at[1], next_q, in_sem.at[6])
+    loads.add("next_o", wo_hbm.at[1], next_o, in_sem.at[7])
     loads.begin()
     pushed = []
 
-    def push(*names):
-        for name in names:
-            index = KEPT.index(name)
-            pushed.append(pltpu.make_async_copy(kept_refs[index], kept_hbm[index], out_sem.at[index]))
+    def push(half, names, sources, targets, sems, wanted):
+        for name in wanted:
+            index = names.index(name)
+            unit = GROWS if name == "probs" else 1
+            rows = pl.ds(half * HALF // unit, HALF // unit)
+            pushed.append(
+                pltpu.make_async_copy(sources[index].at[rows], targets[index].at[rows], sems.at[index, half])
+            )
             pushed[-1].start()
 
     _, _, pick_char, pick_seq = row_choices()
@@ -434,29 +487,45 @@
         [jnp.sin(phase) for phase in cycles] + [jnp.cos(phase) for phase in cycles], axis=1
     ).astype(BF)
     feat_ref[...] = features
-    for copy in brought:
-        copy.wait()
+    while brought:
+        brought.pop().wait()
     loads.need("t")
     xs[...] = nn(pick_char[:, 0:vocab], embed_ref[...]) + time_shift(features, weight.t[...], pick_seq)
-    tasks = forward_tasks(0, small, weight, kept, xs, xs, mid, bias, masks, loads.need)
-    after = {"ln11": ("unit1", "rstd1", "norm1"), "qkv1": ("qkv",), "attend1": ("probs", "att"),
-             "ln21": ("unit2", "rstd2", "norm2"), "up1": ("hid", "slp")}
-    for name in FORWARD_ORDER:
-        tasks[name]()
-        push(*after.get(name, ()))
-    loads.need("later")
-    xs[...] = xs[...] + time_shift(features, later[...], pick_seq)
+    tasks = forward_tasks(0, small, weight, kept, xs, xs, mid, bias, masks, loads.need, brought, shifted)
+
+    def shift_next():
+        loads.need("later")
+        shifted[...] = time_shift(features, later[...], pick_seq)
+
+    tasks["shift0"] = shift_next
+    after = {"ln1": ("unit1", "rstd1", "norm1"), "qkv": ("qkv",), "attend": ("probs", "att"),
+             "ln2": ("unit2", "rstd2", "norm2"), "up": ("hid", "slp")}
+    second = forward_tasks(
+        1, small, SimpleNamespace(q=next_q, o=next_o), early, xs, xs, mid, bias, masks,
+        lambda name: loads.need("next_" + name), brought,
+    )
+    for order, work, target in (
+        (FIRST_ORDER, tasks, (KEPT, kept_refs, kept_hbm, out_sem)),
+        (SECOND_ORDER, second, (EARLY, early_refs, early_hbm, early_sem)),
+    ):
+        for names in order:
+            run_parts(names, work)
+            loads.advance(PER_TASK)
+            for name in names.split("|"):
+                wanted = [array for array in after.get(name[:-1], ()) if array in target[0]]
+                push(int(name[-1]), *target, wanted)
+    loads.need("next_o")
     for copy in pushed:
         copy.wait()
 
 
 def other_layers(
-    own_ref, feat_ref, bias, x_ref, chars_hbm, g1_hbm, b1_hbm, g2_hbm, b2_hbm, eb_hbm,
+    own_ref, feat_ref, x_ref, att_ref, o_ref, chars_hbm, g1_hbm, b1_hbm, g2_hbm, b2_hbm, eb_hbm,
     table_hbm, wt_hbm, wq_hbm, wo_hbm, we_hbm, wc_hbm, *rest, scale
 ):
     count = len(KEPT)
     layers, width = g1_hbm.shape
-    kept_hbm, rest = rest[:count], rest[count:]
+    kept_hbm, early_hbm, rest = rest[:count], rest[count : count + len(EARLY)], rest[count + len(EARLY) :]
     act_hbm, *little_hbm = rest[:7]
     outs = dict(zip(("time", "qkv", "out", "up", "down"), rest[7:12]))
     rest = rest[12:]
@@ -465,13 +534,14 @@
         weights.append(SimpleNamespace(**dict(zip("tqoec", rest[:5]))))
         kept.append(SimpleNamespace(**dict(zip(KEPT, rest[5 : 5 + count]))))
         rest = rest[5 + count :]
+    weights[1].o, kept[1].att = o_ref, att_ref
     names = ("xs", "mid", "acc", "ga", "gproj", "gscore", "gu", "gb", "gff", "end", "act", "table")
     work = SimpleNamespace(**dict(zip(names, rest)))
     rest = rest[len(names) :]
     stages = dict(zip(outs, rest[:5]))
     little, rest = rest[5:11], rest[11:]
     (chars_ref, *smalls), rest = rest[:6], rest[6:]
-    in_sem, kept_sem, out_sem, end_sem, small_sem, little_sem = rest
+    in_sem, kept_sem, early_sem, out_sem, end_sem, small_sem, little_sem = rest
     eg, g1g, b1g, g2g, b2g, ubg = little
     xs, mid = work.xs, work.mid
     small = SimpleNamespace(**dict(zip(SMALLS, smalls)))
@@ -480,10 +550,16 @@
     sources = dict(zip("tqoec", (wt_hbm, wq_hbm, wo_hbm, we_hbm, wc_hbm)))
     loads = Loads(DEPTH)
     for layer in range(1, layers):
-        for index, name in enumerate("tqoec"):
-            if layer == 1 and name == "t":
-                continue
-            loads.add((layer, name), sources[name].at[layer], getattr(weights[layer], name), in_sem.at[index, layer])
+        for name in "ec" if layer == 1 else "tqoec":
+            loads.add(
+                (layer, name), sources[name].at[layer], getattr(weights[layer], name), in_sem.at["tqoec".index(name), layer]
+            )
+    for name in ("probs", "qkv", "norm1", "q", "unit1", "rstd1"):
+        if name in EARLY:
+            index = EARLY.index(name)
+            loads.add((1, name), early_hbm[index], getattr(kept[1], name), early_sem.at[index])
+        else:
+            loads.add((1, name), sources[name].at[1], weights[1].q, in_sem.at["tqoec".index(name), 1])
     for name in ("slp", "c", "hid", "e", "norm2", "unit2", "rstd2", "o", "att", "probs", "qkv", "q", "norm1", "unit1", "rstd1"):
         if name in KEPT:
             index = KEPT.index(name)
@@ -501,16 +577,15 @@
     seq_of, char_of, pick_char, pick_seq = row_choices()
     masks = side_masks()
     features = feat_ref[...]
-    for copy in brought:
-        copy.wait()
     for layer in range(1, layers):
-        source = x_ref if layer == 1 else xs
+        source, order = (x_ref, LATTER_ORDER) if layer == 1 else (xs, FORWARD_ORDER)
         if layer > 1:
             needs(layer)("t")
             xs[...] = xs[...] + time_shift(features, weights[layer].t[...], pick_seq)
         run_tasks(
-            FORWARD_ORDER,
-            forward_tasks(layer, small, weights[layer], kept[layer], source, xs, mid, bias, masks, needs(layer)),
+            order,
+            forward_tasks(layer, small, weights[layer], kept[layer], source, xs, mid, None, masks, needs(layer), brought),
+            loads,
         )
 
     own = own_ref[0]
@@ -532,13 +607,14 @@
 
     sends = {}
 
-    def send(name, layer, value):
+    def send(name, layer, left, right):
         if name in sends:
             sends.pop(name).wait()
-        stages[name][...] = value()
-        copy = pltpu.make_async_copy(
-            stages[name], outs[name].at[layer], out_sem.at[list(outs).index(name), layer]
-        )
+        stage = stages[name]
+        for start in range(0, stage.shape[0], BAND):
+            stage[start : start + BAND, :] = tn(left[:, start : start + BAND], right[...])
+            yield
+        copy = pltpu.make_async_copy(stage, outs[name].at[layer], out_sem.at[list(outs).index(name), layer])
         copy.start()
         sends[name] = copy
 
@@ -547,6 +623,7 @@
             BACKWARD_ORDER,
             backward_tasks(layer, small, weights[layer], kept[layer], work, masks, needs(layer), send,
                            features, (pick_char, pick_seq), grads),
+            loads,
         )
     finals = bring(little, little_hbm, little_sem)
     act_copy.wait()
@@ -590,29 +667,33 @@
     (embed, ln1_gain, ln1_bias, _, _, _, ln2_gain, ln2_bias, _, expand_bias, _) = weights
     width, inner = embed.shape[1], expand_bias.shape[1]
     shapes = kept_shapes(width, inner)
+    early = [shapes[KEPT.index(name)] for name in EARLY]
     table = (NROWS, width)
     smalls = (embed, ln1_gain, ln1_bias, ln2_gain, ln2_bias, expand_bias)
     return call(
         first_layer,
         [
             pltpu.VMEM((CHUNK, width), BF),
+            pltpu.VMEM(table, F32),
+            pltpu.VMEM(table, BF),
+            pltpu.VMEM(big[2].shape[1:], BF),
+        ]
+        + [pltpu.HBM(shape, dtype) for shape, dtype in shapes + early],
+        (counts, *map(far, smalls), *map(far, big)),
+        [vmem()] + [anywhere()] * (6 + len(big)),
+        [vmem()] * 4 + [anywhere()] * (len(shapes) + len(early)),
+        [pltpu.VMEM(w.shape[1:], w.dtype) for w in big]
+        + [pltpu.VMEM(shape, dtype) for shape, dtype in shapes + early]
+        + [pltpu.VMEM(small.shape, BF) for small in smalls]
+        + [
+            pltpu.VMEM(big[0].shape[1:], BF),
+            pltpu.VMEM(big[1].shape[1:], BF),
             pltpu.VMEM((NGROUPS, GROWS, GROWS), F32),
             pltpu.VMEM(table, F32),
-        ]
-        + [pltpu.HBM(shape, dtype) for shape, dtype in shapes],
-        (counts, *map(far, smalls), *map(far, big)),
-        [vmem()] + [anywhere()] * (6 + len(big)),
-        [vmem()] * 3 + [anywhere()] * len(shapes),
-        [pltpu.VMEM(w.shape[1:], w.dtype) for w in big]
-        + [pltpu.VMEM(shape, dtype) for shape, dtype in shapes]
-        + [
-            pltpu.VMEM(small.shape, BF) for small in smalls
-        ]
-        + [
-            pltpu.VMEM(big[0].shape[1:], BF),
             pltpu.VMEM(table, F32),
-            pltpu.SemaphoreType.DMA((len(big) + 1,)),
-            pltpu.SemaphoreType.DMA((len(shapes),)),
+            pltpu.SemaphoreType.DMA((len(big) + 3,)),
+            pltpu.SemaphoreType.DMA((len(shapes), NROWS // HALF)),
+            pltpu.SemaphoreType.DMA((len(early), NROWS // HALF)),
             pltpu.SemaphoreType.DMA((len(smalls),)),
         ],
         name="forward",
@@ -632,7 +713,7 @@
     def f32_like(array):
         return jax.ShapeDtypeStruct(array.shape, F32)
 
-    features, bias, x, *kept = passed
+    features, x, att, next_o, *kept = passed
     layer_scratch = [pltpu.VMEM(w.shape[1:], w.dtype) for w in big] + [
         pltpu.VMEM(shape, dtype) for shape, dtype in shapes
     ]
@@ -642,9 +723,9 @@
         lambda *refs: other_layers(*refs, scale=scale),
         [jax.ShapeDtypeStruct((positions, width), BF)]
         + [f32_like(w) for w in (*little, w_time, w_qkv, w_out, expand_weight, contract_weight)],
-        (own, keep(features), keep(bias), keep(x), far(chars_row), *map(far, smalls), keep(table), *map(far, big),
+        (own, keep(features), keep(x), keep(att), keep(next_o), far(chars_row), *map(far, smalls), keep(table), *map(far, big),
          *map(far, kept)),
-        [smem()] + [vmem()] * 3 + [anywhere()] * (7 + len(big) + len(kept)),
+        [smem()] + [vmem()] * 4 + [anywhere()] * (7 + len(big) + len(kept)),
         [anywhere()] * 12,
         layer_scratch * layers
         + [
@@ -668,6 +749,7 @@
         + [
             pltpu.SemaphoreType.DMA((len(big), layers)),
             pltpu.SemaphoreType.DMA((len(shapes),)),
+            pltpu.SemaphoreType.DMA((len(EARLY),)),
             pltpu.SemaphoreType.DMA((len(big), layers)),
             pltpu.SemaphoreType.DMA((3,)),
             pltpu.SemaphoreType.DMA((1 + len(smalls),)),

time: 70.1 us -> 66.1 us (0.943)
  waiting for transfers between devices: 9.95 us -> 6.49 us
    all_to_all x1, waiting for transfers between devices: 3.46 us -> 0.01 us  [per_device(): table = lax.all_to_all(table, 'dp', split_axis=0, concat_axis=0, tiled=True)]
  transfers between devices with their start and end apart: 3 -> 3, of which waited for: 2 -> 1; matrix products, arithmetic and copies ran while one was open for 0% -> 0% of each run, Pallas kernels for 17% -> 23%
where the time goes in v1:
time: 66.1 us; the launch traced here: 65.7 us
  Pallas kernels  46.3 us (70%)
  starting transfers between devices  11.4 us (17%)
  waiting for transfers between devices  6.49 us (10%)
  between operations  1.52 us (2%)
    pallas_call x4, Pallas kernels, call(): pl.pallas_call(body, out_shape=outs, in_specs=in_specs, out_specs=out_spe...  46.3 us
    all_to_all x1, waiting for transfers between devices, per_device(): lax.all_to_all(counts, ('dp', 'blk'), split_axis=0, concat_axis=0, tiled=...  6.49 us
    all_to_all x1, starting transfers between devices, per_device(): lax.all_to_all(counts, ('dp', 'blk'), split_axis=0, concat_axis=0, tiled=...  4.92 us
    all_to_all x1, starting transfers between devices, per_device(): table = lax.all_to_all(table, 'dp', split_axis=0, concat_axis=0, tiled=True)  3.57 us
    ppermute x1, starting transfers between devices, per_device(): lax.ppermute(sums, 'blk', [(i, (i + step) % n_blk) for i in range(n_blk)])  2.94 us
  transfers between devices with their start and end apart: 3, of which 1 were waited for; matrix products, arithmetic and copies ran while one was open for 0% of the time, Pallas kernels for 23%

profile of v1, /device:TPU:0, one launch (start us, length us, event | category | flops | bytes accessed | tf_op | source)
XLA Modules:
  0.0 65.7 jit_solution(4456243176306596957)
XLA Ops:
  1.3 2.1 %local_sums.1 = (f32[32,1,256]{2,1,0:T(1,128)}, f32[32,512]{1,0:T(8,128)S(1)}) custom-call(s32[1,1024]{1,0:T(1,128)} %bitcast.6, bf16[1024,512]{1,0:T(8,128)(2,1)} %bitcast.5, s32[1]{0:T(128)} %bitcast.3.refs_2_, s32[1]{0:T(128)S(6)} %copy.26.refs_3_), custom_call_target="tpu_custom_call" | custom-call | tf_op jit(solution)/shard_map/local_sums/pallas_call | solution.py:647
  3.4 2.9 %collective-permute-start = (f32[32,512]{1,0:T(8,128)S(1)}, f32[32,512]{1,0:T(8,128)S(1)}, u32[]{:S(2)}, u32[]{:S(2)}) collective-permute-start(f32[32,512]{1,0:T(8,128)S(1)} %get-tuple-element.51.refs_0_), channel_id=1, source_target_pairs={{0,1},{1,0},{2,3},{3,2},{4,5},{5,4},{6,7},{7,6},{8,9},{9,8},{10,11... | collective-permute-start | bytes 196616 | tf_op jit(solution)/shard_map/ppermute | solution.py:791
  6.3 4.9 %all-to-all-start = ((f32[32,1,256]{2,1,0:T(1,128)}), f32[32,1,256]{2,1,0:T(1,128)S(1)}, u32[]{:S(2)}, u32[]{:S(2)}) async-start(f32[32,1,256]{2,1,0:T(1,128)} %get-tuple-element.46), calls=%async_computation | async-start | bytes 65536 | tf_op jit(solution)/shard_map/all_to_all | solution.py:789
  11.3 0.0 collective-permute-done.refs_1_
  11.3 0.9 %spread_sums.1 = bf16[16,32,512]{2,1,0:T(8,128)(2,1)} custom-call(f32[32,512]{1,0:T(8,128)S(1)} %get-tuple-element.51.refs_0_, f32[32,512]{1,0:T(8,128)S(1)} %collective-permute-done.refs_1_), custom_call_target="tpu_custom_call" | custom-call | tf_op jit(solution)/shard_map/spread_sums/pallas_call | solution.py:647
  12.1 6.5 %all-to-all-done.counts_ref = f32[32,1,256]{2,1,0:T(1,128)S(1)} async-done(((f32[32,1,256]{2,1,0:T(1,128)}), f32[32,1,256]{2,1,0:T(1,128)S(1)}, u32[]{:S(2)}, u32[]{:S(2)}) %all-to-all-start) | async-done | bytes 32800 | tf_op jit(solution)/shard_map/all_to_all | solution.py:789
  18.6 3.6 %all-to-all-start.1 = ((bf16[16,32,512]{2,1,0:T(8,128)(2,1)}), bf16[16,32,512]{2,1,0:T(8,128)(2,1)S(1)}, u32[]{:S(2)}, u32[]{:S(2)}) async-start(bf16[16,32,512]{2,1,0:T(8,128)(2,1)} %spread_sums.1), calls=%async_computation.1 | async-start | bytes 1048576 | tf_op jit(solution)/shard_map/all_to_all | solution.py:802
  22.2 14.5 %forward.1 = (bf16[16,512]{1,0:T(8,128)(2,1)S(1)}, f32[448,512]{1,0:T(8,128)S(1)}, bf16[448,512]{1,0:T(8,128)(2,1)S(1)}, bf16[512,512]{1,0:T(8,128)(2,1)S(1)}, b...) custom-call(f32[32,1,256]{2,1,0:T(1,128)S(1)} %all-to-all-done.count, ...), custom_call_target="tpu_custom_call" | custom-call | tf_op jit(solution)/shard_map/forward/pallas_call | solution.py:647
  36.7 0.0 all-to-all-done.1.refs_11_
  36.7 28.9 %backward.1 = (bf16[1024,512]{1,0:T(8,128)(2,1)}, f32[27,512]{1,0:T(8,128)}, f32[2,512]{1,0:T(2,128)}, f32[2,512]{1,0:T(2,128)}, f32[2,512]{1,0:T(2,128)}, /*ind...) custom-call(s32[1]{0:T(128)} %bitcast.refs_0_, ...), custom_call_target="tpu_custom_call" | custom-call | tf_op jit(solution)/shard_map/backward/pallas_call | solution.py:647
Async XLA Ops:
  3.4 7.9 %collective-permute-start = (f32[32,512]{1,0:T(8,128)S(1)}, f32[32,512]{1,0:T(8,128)S(1)}, u32[]{:S(2)}, u32[]{:S(2)}) collective-permute-start(f32[32,512]{1,0:T(8,128)S(1)} %get-tuple-element.51.refs_0_), channel_id=1, source_target_pairs={{0,1},{1,0},{2,3},{3,2},{4,5},{5,4},{6,7},{7,6},{8,9},{9,8},{10,11... | collective-permute-start | bytes 196616 | tf_op jit(solution)/shard_map/ppermute | solution.py:791
  6.3 12.3 %all-to-all-start = ((f32[32,1,256]{2,1,0:T(1,128)}), f32[32,1,256]{2,1,0:T(1,128)S(1)}, u32[]{:S(2)}, u32[]{:S(2)}) async-start(f32[32,1,256]{2,1,0:T(1,128)} %get-tuple-element.46), calls=%async_computation | async-start | bytes 65536 | tf_op jit(solution)/shard_map/all_to_all | solution.py:789
  18.6 18.1 %all-to-all-start.1 = ((bf16[16,32,512]{2,1,0:T(8,128)(2,1)}), bf16[16,32,512]{2,1,0:T(8,128)(2,1)S(1)}, u32[]{:S(2)}, u32[]{:S(2)}) async-start(bf16[16,32,512]{2,1,0:T(8,128)(2,1)} %spread_sums.1), calls=%async_computation.1 | async-start | bytes 1048576 | tf_op jit(solution)/shard_map/all_to_all | solution.py:802

commit v2 on v1

--- a/solution.py
+++ b/solution.py
@@ -72,12 +72,21 @@
 
 
 def spread_sums(*refs):
-    total = refs[0][...]
-    for ref in refs[1:-1]:
+    *parts, embed, g1, b1, g2, b2, eb, out, pack = refs
+    total = parts[0][...]
+    for ref in parts[1:]:
         total = total + ref[...]
     total = total.astype(BF)
-    for device in range(refs[-1].shape[0]):
-        refs[-1][device] = total
+    for device in range(out.shape[0]):
+        out[device] = total
+    layers, width = g1.shape
+    row = 0
+    for ref in (g1, b1, g2, b2, eb):
+        for layer in range(layers):
+            for start in range(0, ref.shape[1], width):
+                pack[row : row + 1, :] = ref[layer : layer + 1, start : start + width].astype(F32)
+                row += 1
+    pack[row : row + embed.shape[0], :] = embed[...].astype(F32)
 
 
 class Loads:
@@ -155,8 +164,14 @@
     return jnp.concatenate([both * masks[0], both * masks[1]], axis=0)
 
 
-def wide(ref, layer):
-    return ref[layer : layer + 1, :].astype(F32)
+def wide(rows, layer):
+    pack, first = rows
+    return pack[first + layer : first + layer + 1, :]
+
+
+def small_rows(pack, layers, pieces):
+    firsts = dict(g1=0, b1=layers, g2=2 * layers, b2=3 * layers, eb=4 * layers, embed=(4 + pieces) * layers)
+    return SimpleNamespace(**{name: (pack, first) for name, first in firsts.items()})
 
 
 EARLY = ("unit1", "rstd1", "norm1", "qkv", "probs")
@@ -182,15 +197,13 @@
     return range(span.start // GROWS, span.stop // GROWS)
 
 
-def forward_tasks(layer, small, weight, kept, source, xs, mid, bias, masks, need, brought, shifted=None):
+def forward_tasks(layer, small, weight, kept, source, xs, mid, bias, masks, need, shifted=None):
     width = xs.shape[1]
     inner = kept.hid.shape[1]
     pairs = width // KPAD
 
     def normed(span, values, unit_ref, rstd_ref, norm_ref, gain, shift):
         unit, rstd = normalise(values[span, :])
-        while brought:
-            brought.pop().wait()
         unit_ref[span, :] = unit.astype(BF)
         rstd_ref[span, :] = jnp.broadcast_to(rstd, (rstd.shape[0], KPAD))
         norm_ref[span, :] = (unit * wide(gain, layer) + wide(shift, layer)).astype(BF)
@@ -239,7 +252,7 @@
         for piece in range(inner // PIECE):
             cols = slice(piece * PIECE, (piece + 1) * PIECE)
             product = nn(kept.norm2[span, :], weight.e[:, cols])
-            shift = small.eb[layer : layer + 1, cols].astype(F32)
+            shift = wide(small.eb, layer * (inner // PIECE) + piece)
             for rows in strips(span, GSTRIP):
                 strip = product[rows.start - span.start : rows.stop - span.start]
                 hidden, slope = gelu_and_slope(strip + shift)
@@ -392,11 +405,9 @@
     "ln10", "ln11", "qkv0", "qkv1", "attend0", "out0", "ln20", "attend1|up0", "out1", "ln21", "down0|up1", "down1",
 )
 BACKWARD_ORDER = (
-    "down_term", "grad_up0", "up_term", "grad_norm20", "ln2_back0", "out_term", "grad_att0", "attend_back0", "qkv_term", "grad_norm10", "ln1_back0", "time_term",
+    "grad_up0", "down_term", "grad_norm20", "ln2_back0|up_term", "grad_att0", "attend_back0|out_term", "grad_norm10",
+    "ln1_back0|qkv_term", "time_term",
 )
-
-
-SMALLS = ("g1", "b1", "g2", "b2", "eb")
 
 
 def bring(sources, targets, sems):
@@ -423,9 +434,9 @@
 
 
 def first_layer(
-    counts_ref, embed_hbm, g1_hbm, b1_hbm, g2_hbm, b2_hbm, eb_hbm,
+    counts_ref, pack_ref,
     wt_hbm, wq_hbm, wo_hbm, we_hbm, wc_hbm,
-    feat_ref, xs, next_att, next_o, *rest
+    feat_ref, xs, next_att, next_o, *rest, vocab
 ):
     count = len(KEPT)
     kept_hbm, early_hbm, rest = rest[:count], rest[count : count + len(EARLY)], rest[count + len(EARLY) :]
@@ -434,12 +445,9 @@
     kept = SimpleNamespace(**dict(zip(KEPT, kept_refs)))
     early_refs, rest = rest[: len(EARLY)], rest[len(EARLY) :]
     early = SimpleNamespace(att=next_att, hid=kept.hid, **dict(zip(EARLY, early_refs)))
-    embed_ref, *smalls = rest[:6]
-    later, next_q, bias, mid, shifted, in_sem, out_sem, early_sem, small_sem = rest[6:]
+    later, next_q, bias, mid, shifted, in_sem, out_sem, early_sem = rest
     width = xs.shape[1]
-    vocab = embed_ref.shape[0]
-    small = SimpleNamespace(**dict(zip(SMALLS, smalls)))
-    brought = bring((embed_hbm, g1_hbm, b1_hbm, g2_hbm, b2_hbm, eb_hbm), (embed_ref, *smalls), small_sem)
+    small = small_rows(pack_ref, wt_hbm.shape[0], kept.hid.shape[1] // PIECE)
     loads = Loads(2)
     for index, (name, source) in enumerate(zip("tqoec", (wt_hbm, wq_hbm, wo_hbm, we_hbm, wc_hbm))):
         loads.add(name, source.at[0], getattr(weight, name), in_sem.at[index])
@@ -487,11 +495,10 @@
         [jnp.sin(phase) for phase in cycles] + [jnp.cos(phase) for phase in cycles], axis=1
     ).astype(BF)
     feat_ref[...] = features
-    while brought:
-        brought.pop().wait()
     loads.need("t")
-    xs[...] = nn(pick_char[:, 0:vocab], embed_ref[...]) + time_shift(features, weight.t[...], pick_seq)
-    tasks = forward_tasks(0, small, weight, kept, xs, xs, mid, bias, masks, loads.need, brought, shifted)
+    embed = pack_ref[small.embed[1] : small.embed[1] + vocab, :].astype(BF)
+    xs[...] = nn(pick_char[:, 0:vocab], embed) + time_shift(features, weight.t[...], pick_seq)
+    tasks = forward_tasks(0, small, weight, kept, xs, xs, mid, bias, masks, loads.need, shifted)
 
     def shift_next():
         loads.need("later")
@@ -502,7 +509,7 @@
              "ln2": ("unit2", "rstd2", "norm2"), "up": ("hid", "slp")}
     second = forward_tasks(
         1, small, SimpleNamespace(q=next_q, o=next_o), early, xs, xs, mid, bias, masks,
-        lambda name: loads.need("next_" + name), brought,
+        lambda name: loads.need("next_" + name),
     )
     for order, work, target in (
         (FIRST_ORDER, tasks, (KEPT, kept_refs, kept_hbm, out_sem)),
@@ -520,11 +527,11 @@
 
 
 def other_layers(
-    own_ref, feat_ref, x_ref, att_ref, o_ref, chars_hbm, g1_hbm, b1_hbm, g2_hbm, b2_hbm, eb_hbm,
+    own_ref, feat_ref, x_ref, att_ref, o_ref, pack_ref, chars_hbm,
     table_hbm, wt_hbm, wq_hbm, wo_hbm, we_hbm, wc_hbm, *rest, scale
 ):
     count = len(KEPT)
-    layers, width = g1_hbm.shape
+    layers, width = wq_hbm.shape[:2]
     kept_hbm, early_hbm, rest = rest[:count], rest[count : count + len(EARLY)], rest[count + len(EARLY) :]
     act_hbm, *little_hbm = rest[:7]
     outs = dict(zip(("time", "qkv", "out", "up", "down"), rest[7:12]))
@@ -540,12 +547,12 @@
     rest = rest[len(names) :]
     stages = dict(zip(outs, rest[:5]))
     little, rest = rest[5:11], rest[11:]
-    (chars_ref, *smalls), rest = rest[:6], rest[6:]
+    chars_ref, rest = rest[0], rest[1:]
     in_sem, kept_sem, early_sem, out_sem, end_sem, small_sem, little_sem = rest
     eg, g1g, b1g, g2g, b2g, ubg = little
     xs, mid = work.xs, work.mid
-    small = SimpleNamespace(**dict(zip(SMALLS, smalls)))
-    brought = bring((chars_hbm, g1_hbm, b1_hbm, g2_hbm, b2_hbm, eb_hbm), (chars_ref, *smalls), small_sem)
+    small = small_rows(pack_ref, layers, kept[0].hid.shape[1] // PIECE)
+    (chars_copy,) = bring((chars_hbm,), (chars_ref,), small_sem)
     grads = SimpleNamespace(eg=eg, g1=g1g, b1=b1g, g2=g2g, b2=b2g, ub=ubg)
     sources = dict(zip("tqoec", (wt_hbm, wq_hbm, wo_hbm, we_hbm, wc_hbm)))
     loads = Loads(DEPTH)
@@ -584,13 +591,14 @@
             xs[...] = xs[...] + time_shift(features, weights[layer].t[...], pick_seq)
         run_tasks(
             order,
-            forward_tasks(layer, small, weights[layer], kept[layer], source, xs, mid, None, masks, needs(layer), brought),
+            forward_tasks(layer, small, weights[layer], kept[layer], source, xs, mid, None, masks, needs(layer)),
             loads,
         )
 
     own = own_ref[0]
     work.end[0:NROWS, :] = xs[...].astype(BF)
     work.end[NROWS:, :] = jnp.zeros((work.end.shape[0] - NROWS, width), BF)
+    chars_copy.wait()
     place = chars_ref[...] + lax.rem(own, GROUP) * ROWS
     hot = (place == iota((KPAD, chars_ref.shape[1]), 0)).astype(F32).astype(BF)
     start = pl.multiple_of(lax.div(own, GROUP) * GROWS, 16)
@@ -598,12 +606,10 @@
     act_copy = pltpu.make_async_copy(work.act, act_hbm, end_sem.at[1])
     act_copy.start()
 
-    slot_row = seq_of * SLOT + char_of
-    spread = (slot_row == iota((NROWS, CHUNK * SLOT), 1)).astype(F32).astype(BF)
     table_copy.wait()
-    incoming = nn(spread, work.table[...].reshape(CHUNK * SLOT, width)) * scale
-    xs[...] = incoming
-    work.gff[...] = incoming.astype(BF)
+    for seq in range(CHUNK):
+        xs[seq * ROWS : (seq + 1) * ROWS, :] = work.table[seq].astype(F32)[0:ROWS] * scale
+    work.gff[...] = xs[...].astype(BF)
 
     sends = {}
 
@@ -663,15 +669,14 @@
     return pltpu.with_memory_space_constraint(array, pltpu.VMEM)
 
 
-def run_forward(counts, weights, big):
-    (embed, ln1_gain, ln1_bias, _, _, _, ln2_gain, ln2_bias, _, expand_bias, _) = weights
+def run_forward(counts, pack, weights, big):
+    embed, expand_bias = weights[0], weights[9]
     width, inner = embed.shape[1], expand_bias.shape[1]
     shapes = kept_shapes(width, inner)
     early = [shapes[KEPT.index(name)] for name in EARLY]
     table = (NROWS, width)
-    smalls = (embed, ln1_gain, ln1_bias, ln2_gain, ln2_bias, expand_bias)
     return call(
-        first_layer,
+        lambda *refs: first_layer(*refs, vocab=embed.shape[0]),
         [
             pltpu.VMEM((CHUNK, width), BF),
             pltpu.VMEM(table, F32),
@@ -679,12 +684,11 @@
             pltpu.VMEM(big[2].shape[1:], BF),
         ]
         + [pltpu.HBM(shape, dtype) for shape, dtype in shapes + early],
-        (counts, *map(far, smalls), *map(far, big)),
-        [vmem()] + [anywhere()] * (6 + len(big)),
+        (counts, keep(pack), *map(far, big)),
+        [vmem()] * 2 + [anywhere()] * len(big),
         [vmem()] * 4 + [anywhere()] * (len(shapes) + len(early)),
         [pltpu.VMEM(w.shape[1:], w.dtype) for w in big]
         + [pltpu.VMEM(shape, dtype) for shape, dtype in shapes + early]
-        + [pltpu.VMEM(small.shape, BF) for small in smalls]
         + [
             pltpu.VMEM(big[0].shape[1:], BF),
             pltpu.VMEM(big[1].shape[1:], BF),
@@ -694,14 +698,13 @@
             pltpu.SemaphoreType.DMA((len(big) + 3,)),
             pltpu.SemaphoreType.DMA((len(shapes), NROWS // HALF)),
             pltpu.SemaphoreType.DMA((len(early), NROWS // HALF)),
-            pltpu.SemaphoreType.DMA((len(smalls),)),
         ],
         name="forward",
         mib=40,
     )
 
 
-def run_backward(own, chars_row, table, weights, big, passed, scale):
+def run_backward(own, chars_row, pack, table, weights, big, passed, scale):
     (embed, ln1_gain, ln1_bias, w_time, w_qkv, w_out, ln2_gain, ln2_bias, expand_weight, expand_bias,
      contract_weight) = weights
     layers, width = ln1_gain.shape
@@ -723,9 +726,9 @@
         lambda *refs: other_layers(*refs, scale=scale),
         [jax.ShapeDtypeStruct((positions, width), BF)]
         + [f32_like(w) for w in (*little, w_time, w_qkv, w_out, expand_weight, contract_weight)],
-        (own, keep(features), keep(x), keep(att), keep(next_o), far(chars_row), *map(far, smalls), keep(table), *map(far, big),
+        (own, keep(features), keep(x), keep(att), keep(next_o), keep(pack), far(chars_row), keep(table), *map(far, big),
          *map(far, kept)),
-        [smem()] + [vmem()] * 4 + [anywhere()] * (7 + len(big) + len(kept)),
+        [smem()] + [vmem()] * 5 + [anywhere()] * (2 + len(big) + len(kept)),
         [anywhere()] * 12,
         layer_scratch * layers
         + [
@@ -745,14 +748,13 @@
         + [pltpu.VMEM(w.shape[1:], F32) for w in big]
         + [pltpu.VMEM(w.shape, F32) for w in little]
         + [pltpu.VMEM(chars_row.shape, I32)]
-        + [pltpu.VMEM(small.shape, BF) for small in smalls]
         + [
             pltpu.SemaphoreType.DMA((len(big), layers)),
             pltpu.SemaphoreType.DMA((len(shapes),)),
             pltpu.SemaphoreType.DMA((len(EARLY),)),
             pltpu.SemaphoreType.DMA((len(big), layers)),
             pltpu.SemaphoreType.DMA((3,)),
-            pltpu.SemaphoreType.DMA((1 + len(smalls),)),
+            pltpu.SemaphoreType.DMA((1,)),
             pltpu.SemaphoreType.DMA((len(little),)),
         ],
         name="backward",
@@ -773,8 +775,8 @@
     counts, sums = call(
         lambda *refs: local_sums(*refs, shares=n_blk),
         [
-            jax.ShapeDtypeStruct((n_dp * n_blk, 1, 2 * KPAD), F32),
-            jax.ShapeDtypeStruct((SLOT, width), F32),
+            pltpu.VMEM((n_dp * n_blk, 1, 2 * KPAD), F32),
+            pltpu.VMEM((SLOT, width), F32),
         ],
         (
             far(chars_row),
@@ -791,19 +793,25 @@
         lax.ppermute(sums, "blk", [(i, (i + step) % n_blk) for i in range(n_blk)])
         for step in range(1, n_blk)
     ]
-    table = call(
+    embed, ln1_gain, ln1_bias, _, _, _, ln2_gain, ln2_bias, _, expand_bias, _ = weights
+    smalls = (embed, ln1_gain, ln1_bias, ln2_gain, ln2_bias, expand_bias)
+    pack_rows = sum(w.size for w in smalls) // width
+    table, pack = call(
         spread_sums,
-        jax.ShapeDtypeStruct((n_dp, SLOT, width), BF),
-        parts,
-        [vmem()] * len(parts),
-        vmem(),
+        [
+            pltpu.VMEM((n_dp, SLOT, width), BF) if n_dp == CHUNK else jax.ShapeDtypeStruct((n_dp, SLOT, width), BF),
+            pltpu.VMEM((pack_rows + -pack_rows % 8, width), F32),
+        ],
+        (*parts, *map(far, smalls)),
+        [vmem()] * (len(parts) + len(smalls)),
+        [vmem()] * 2,
         name="spread_sums",
     )
     table = lax.all_to_all(table, "dp", split_axis=0, concat_axis=0, tiled=True)
     scale = 1.0 / (n_dp * n_blk)
     if n_dp == CHUNK:
-        kept = run_forward(counts, weights, big)
-        act, grads = run_backward(seq.reshape(1).astype(I32), chars_row, table, weights, big, kept, scale)
+        kept = run_forward(counts, pack, weights, big)
+        act, grads = run_backward(seq.reshape(1).astype(I32), chars_row, pack, table, weights, big, kept, scale)
     else:
 
         def step(carry, chunk):
@@ -813,8 +821,8 @@
             here = lax.dynamic_slice_in_dim(counts, chunk * CHUNK * n_blk, CHUNK * n_blk, axis=0)
             part = lax.dynamic_slice_in_dim(table, chunk * CHUNK, CHUNK, axis=0)
             own = jnp.clip(place, 0, CHUNK - 1).reshape(1).astype(I32)
-            kept = run_forward(here, weights, big)
-            new_act, new_grads = run_backward(own, chars_row, part, weights, big, kept, scale)
+            kept = run_forward(here, pack, weights, big)
+            new_act, new_grads = run_backward(own, chars_row, pack, part, weights, big, kept, scale)
             return (jnp.where(inside, new_act, act), tuple(a + b for a, b in zip(grads, new_grads))), None
 
         start = (jnp.zeros((positions, width), BF), tuple(jnp.zeros(w.shape, F32) for w in weights))

time: 66.1 us -> 65.5 us (level)
    all_to_all x1, waiting for transfers between devices: 6.49 us -> 5.69 us  [per_device(): lax.all_to_all(counts, ('dp', 'blk'), split_axis=0, concat_axis=0, tiled=...]
  transfers between devices with their start and end apart: 3 -> 3, of which waited for: 1 -> 2; matrix products, arithmetic and copies ran while one was open for 0% -> 0% of each run, Pallas kernels for 23% -> 24%
where the time goes in v2:
time: 65.5 us; the launch traced here: 65.1 us
  Pallas kernels  46 us (70%)
  starting transfers between devices  11.4 us (17%)
  waiting for transfers between devices  6.2 us (9%)
  between operations  1.52 us (2%)
    pallas_call x4, Pallas kernels, call(): pl.pallas_call(body, out_shape=outs, in_specs=in_specs, out_specs=out_spe...  46 us
    all_to_all x1, waiting for transfers between devices, per_device(): lax.all_to_all(counts, ('dp', 'blk'), split_axis=0, concat_axis=0, tiled=...  5.69 us
    all_to_all x1, starting transfers between devices, per_device(): lax.all_to_all(counts, ('dp', 'blk'), split_axis=0, concat_axis=0, tiled=...  4.92 us
    all_to_all x1, starting transfers between devices, per_device(): table = lax.all_to_all(table, 'dp', split_axis=0, concat_axis=0, tiled=True)  3.57 us
    ppermute x1, starting transfers between devices, per_device(): lax.ppermute(sums, 'blk', [(i, (i + step) % n_blk) for i in range(n_blk)])  2.94 us
  transfers between devices with their start and end apart: 3, of which 2 were waited for; matrix products, arithmetic and copies ran while one was open for 0% of the time, Pallas kernels for 24%

profile of v2, /device:TPU:0, one launch (start us, length us, event | category | flops | bytes accessed | tf_op | source)
XLA Modules:
  0.0 65.1 jit_solution(8641362097185557679)
XLA Ops:
  1.3 2.1 %local_sums.1 = (f32[32,1,256]{2,1,0:T(1,128)}, f32[32,512]{1,0:T(8,128)S(1)}) custom-call(s32[1,1024]{1,0:T(1,128)} %bitcast.6, bf16[1024,512]{1,0:T(8,128)(2,1)} %bitcast.5, s32[1]{0:T(128)} %bitcast.3.refs_2_, s32[1]{0:T(128)S(6)} %copy.26.refs_3_), custom_call_target="tpu_custom_call" | custom-call | tf_op jit(solution)/shard_map/local_sums/pallas_call | solution.py:653
  3.4 2.9 %collective-permute-start = (f32[32,512]{1,0:T(8,128)S(1)}, f32[32,512]{1,0:T(8,128)S(1)}, u32[]{:S(2)}, u32[]{:S(2)}) collective-permute-start(f32[32,512]{1,0:T(8,128)S(1)} %get-tuple-element.49.refs_0_), channel_id=1, source_target_pairs={{0,1},{1,0},{2,3},{3,2},{4,5},{5,4},{6,7},{7,6},{8,9},{9,8},{10,11... | collective-permute-start | bytes 196616 | tf_op jit(solution)/shard_map/ppermute | solution.py:793
  6.3 4.9 %all-to-all-start = ((f32[32,1,256]{2,1,0:T(1,128)}), f32[32,1,256]{2,1,0:T(1,128)S(1)}, u32[]{:S(2)}, u32[]{:S(2)}) async-start(f32[32,1,256]{2,1,0:T(1,128)} %get-tuple-element.48), calls=%async_computation | async-start | bytes 65536 | tf_op jit(solution)/shard_map/all_to_all | solution.py:791
  11.3 0.0 collective-permute-done.refs_1_
  11.3 1.6 %spread_sums.1 = (bf16[16,32,512]{2,1,0:T(8,128)(2,1)}, f32[48,512]{1,0:T(8,128)S(1)}) custom-call(f32[32,512]{1,0:T(8,128)S(1)} %get-tuple-element.49.refs_0_, f32[32,512]{1,0:T(8,128)S(1)} %collective-permute-done.refs_1_, bf16[27,512]{1,0:T(8,128)(2,1)} %refs_2_.2, bf16[2,512]{1,0:T(2,128)(2,1)} %refs_3_.3, bf16[2,512]{1,0:T(2,128)(2,1)} %refs_4_.2, ...), custom_call_target="tpu_custom_call" | custom-call | tf_op jit(solution)/shard_map/spread_sums/pallas_call | solution.py:653
  12.9 5.7 %all-to-all-done.refs_0_ = f32[32,1,256]{2,1,0:T(1,128)S(1)} async-done(((f32[32,1,256]{2,1,0:T(1,128)}), f32[32,1,256]{2,1,0:T(1,128)S(1)}, u32[]{:S(2)}, u32[]{:S(2)}) %all-to-all-start) | async-done | bytes 32800 | tf_op jit(solution)/shard_map/all_to_all | solution.py:791
  18.6 3.6 %all-to-all-start.1 = ((bf16[16,32,512]{2,1,0:T(8,128)(2,1)}), bf16[16,32,512]{2,1,0:T(8,128)(2,1)S(1)}, u32[]{:S(2)}, u32[]{:S(2)}) async-start(bf16[16,32,512]{2,1,0:T(8,128)(2,1)} %get-tuple-element.55), calls=%async_computation.1 | async-start | bytes 1048576 | tf_op jit(solution)/shard_map/all_to_all | solution.py:810
  22.2 13.9 %forward.1 = (bf16[16,512]{1,0:T(8,128)(2,1)S(1)}, f32[448,512]{1,0:T(8,128)S(1)}, bf16[448,512]{1,0:T(8,128)(2,1)S(1)}, bf16[512,512]{1,0:T(8,128)(2,1)S(1)}, b...) custom-call(f32[32,1,256]{2,1,0:T(1,128)S(1)} %all-to-all-done.refs_, ...), custom_call_target="tpu_custom_call" | custom-call | tf_op jit(solution)/shard_map/forward/pallas_call | solution.py:653
  36.1 0.5 all-to-all-done.1.refs_7_
  36.6 28.3 %backward.1 = (bf16[1024,512]{1,0:T(8,128)(2,1)}, f32[27,512]{1,0:T(8,128)}, f32[2,512]{1,0:T(2,128)}, f32[2,512]{1,0:T(2,128)}, f32[2,512]{1,0:T(2,128)}, /*ind...) custom-call(s32[1]{0:T(128)} %bitcast.refs_0_, ...), custom_call_target="tpu_custom_call" | custom-call | tf_op jit(solution)/shard_map/backward/pallas_call | solution.py:653
Async XLA Ops:
  3.4 7.9 %collective-permute-start = (f32[32,512]{1,0:T(8,128)S(1)}, f32[32,512]{1,0:T(8,128)S(1)}, u32[]{:S(2)}, u32[]{:S(2)}) collective-permute-start(f32[32,512]{1,0:T(8,128)S(1)} %get-tuple-element.49.refs_0_), channel_id=1, source_target_pairs={{0,1},{1,0},{2,3},{3,2},{4,5},{5,4},{6,7},{7,6},{8,9},{9,8},{10,11... | collective-permute-start | bytes 196616 | tf_op jit(solution)/shard_map/ppermute | solution.py:793
  6.3 12.3 %all-to-all-start = ((f32[32,1,256]{2,1,0:T(1,128)}), f32[32,1,256]{2,1,0:T(1,128)S(1)}, u32[]{:S(2)}, u32[]{:S(2)}) async-start(f32[32,1,256]{2,1,0:T(1,128)} %get-tuple-element.48), calls=%async_computation | async-start | bytes 65536 | tf_op jit(solution)/shard_map/all_to_all | solution.py:791
  18.6 18.0 %all-to-all-start.1 = ((bf16[16,32,512]{2,1,0:T(8,128)(2,1)}), bf16[16,32,512]{2,1,0:T(8,128)(2,1)S(1)}, u32[]{:S(2)}, u32[]{:S(2)}) async-start(bf16[16,32,512]{2,1,0:T(8,128)(2,1)} %get-tuple-element.55), calls=%async_computation.1 | async-start | bytes 1048576 | tf_op jit(solution)/shard_map/all_to_all | solution.py:810

commit v3 on v2

--- a/solution.py
+++ b/solution.py
@@ -25,7 +25,7 @@
 F32 = jnp.float32
 I32 = jnp.int32
 MIB = 2**20
-DEPTH = 2
+DEPTH = 3
 GSTRIP = 112
 NSTRIP = 112
 WIDE = 256
@@ -64,7 +64,7 @@
     placed = (chars + place_ref[0] * ROWS == iota((KPAD, positions), 0)).astype(F32)
     counts = nt(jnp.ones((8, positions), BF), placed.astype(BF))[0:1]
     stamp = jnp.full((1, KPAD), time_ref[0].astype(F32) * (1.0 / shares), F32)
-    row = jnp.concatenate([counts, stamp], axis=1)
+    row = jnp.where(iota((1, KPAD), 1) < GROWS, counts, stamp)
     for device in range(count_ref.shape[0]):
         count_ref[device] = row
     onehot = (chars == iota((SLOT, positions), 0)).astype(F32)
@@ -476,11 +476,11 @@
     for group in range(NGROUPS):
         total = jnp.zeros((1, KPAD), F32)
         for member in range(GROUP):
-            value = jnp.zeros((1, 2 * KPAD), F32)
+            value = jnp.zeros((1, KPAD), F32)
             for share in range(shares):
                 value = value + counts_ref[(group * GROUP + member) * shares + share]
-            total = total + value[:, 0:KPAD]
-            stamp.append(value[:, KPAD:])
+            total = total + value
+            stamp.append(jnp.broadcast_to(value[:, GROWS : GROWS + 1], (1, KPAD)))
         same = row_seq(iota((GROWS, GROWS), 1)) == row_seq(iota((GROWS, GROWS), 0))
         counts = jnp.broadcast_to(total[:, 0:GROWS], (GROWS, GROWS)).T
         live = same & (counts > 0.5)
@@ -775,7 +775,7 @@
     counts, sums = call(
         lambda *refs: local_sums(*refs, shares=n_blk),
         [
-            pltpu.VMEM((n_dp * n_blk, 1, 2 * KPAD), F32),
+            pltpu.VMEM((n_dp * n_blk, 1, KPAD), F32),
             pltpu.VMEM((SLOT, width), F32),
         ],
         (

time: 65.5 us -> 65.2 us (level)
  no operation moved by 1% of the time
where the time goes in v3:
time: 65.2 us; the launch traced here: 64.9 us
  Pallas kernels  45.9 us (70%)
  starting transfers between devices  11.4 us (17%)
  waiting for transfers between devices  5.97 us (9%)
  between operations  1.52 us (2%)
    pallas_call x4, Pallas kernels, call(): pl.pallas_call(body, out_shape=outs, in_specs=in_specs, out_specs=out_spe...  45.9 us
    all_to_all x1, waiting for transfers between devices, per_device(): lax.all_to_all(counts, ('dp', 'blk'), split_axis=0, concat_axis=0, tiled=...  5.46 us
    all_to_all x1, starting transfers between devices, per_device(): lax.all_to_all(counts, ('dp', 'blk'), split_axis=0, concat_axis=0, tiled=...  4.92 us
    all_to_all x1, starting transfers between devices, per_device(): table = lax.all_to_all(table, 'dp', split_axis=0, concat_axis=0, tiled=True)  3.57 us
    ppermute x1, starting transfers between devices, per_device(): lax.ppermute(sums, 'blk', [(i, (i + step) % n_blk) for i in range(n_blk)])  2.94 us
  transfers between devices with their start and end apart: 3, of which 2 were waited for; matrix products, arithmetic and copies ran while one was open for 0% of the time, Pallas kernels for 24%

profile of v3, /device:TPU:0, one launch (start us, length us, event | category | flops | bytes accessed | tf_op | source)
XLA Modules:
  0.0 64.9 jit_solution(9741819140221028062)
XLA Ops:
  1.3 2.1 %local_sums.1 = (f32[32,1,128]{2,1,0:T(1,128)}, f32[32,512]{1,0:T(8,128)S(1)}) custom-call(s32[1,1024]{1,0:T(1,128)} %bitcast.6, bf16[1024,512]{1,0:T(8,128)(2,1)} %bitcast.5, s32[1]{0:T(128)} %bitcast.3.refs_2_, s32[1]{0:T(128)S(6)} %copy.26.refs_3_), custom_call_target="tpu_custom_call" | custom-call | tf_op jit(solution)/shard_map/local_sums/pallas_call | solution.py:653
  3.4 2.9 %collective-permute-start = (f32[32,512]{1,0:T(8,128)S(1)}, f32[32,512]{1,0:T(8,128)S(1)}, u32[]{:S(2)}, u32[]{:S(2)}) collective-permute-start(f32[32,512]{1,0:T(8,128)S(1)} %get-tuple-element.49.refs_0_), channel_id=1, source_target_pairs={{0,1},{1,0},{2,3},{3,2},{4,5},{5,4},{6,7},{7,6},{8,9},{9,8},{10,11... | collective-permute-start | bytes 196616 | tf_op jit(solution)/shard_map/ppermute | solution.py:793
  6.3 4.9 %all-to-all-start = ((f32[32,1,128]{2,1,0:T(1,128)}), f32[32,1,128]{2,1,0:T(1,128)S(1)}, u32[]{:S(2)}, u32[]{:S(2)}) async-start(f32[32,1,128]{2,1,0:T(1,128)} %get-tuple-element.48), calls=%async_computation | async-start | bytes 32768 | tf_op jit(solution)/shard_map/all_to_all | solution.py:791
  11.3 0.0 collective-permute-done.refs_1_
  11.3 1.6 %spread_sums.1 = (bf16[16,32,512]{2,1,0:T(8,128)(2,1)}, f32[48,512]{1,0:T(8,128)S(1)}) custom-call(f32[32,512]{1,0:T(8,128)S(1)} %get-tuple-element.49.refs_0_, f32[32,512]{1,0:T(8,128)S(1)} %collective-permute-done.refs_1_, bf16[27,512]{1,0:T(8,128)(2,1)} %refs_2_.2, bf16[2,512]{1,0:T(2,128)(2,1)} %refs_3_.3, bf16[2,512]{1,0:T(2,128)(2,1)} %refs_4_.2, ...), custom_call_target="tpu_custom_call" | custom-call | tf_op jit(solution)/shard_map/spread_sums/pallas_call | solution.py:653
  12.9 5.5 %all-to-all-done.refs_0_ = f32[32,1,128]{2,1,0:T(1,128)S(1)} async-done(((f32[32,1,128]{2,1,0:T(1,128)}), f32[32,1,128]{2,1,0:T(1,128)S(1)}, u32[]{:S(2)}, u32[]{:S(2)}) %all-to-all-start) | async-done | bytes 16416 | tf_op jit(solution)/shard_map/all_to_all | solution.py:791
  18.4 3.6 %all-to-all-start.1 = ((bf16[16,32,512]{2,1,0:T(8,128)(2,1)}), bf16[16,32,512]{2,1,0:T(8,128)(2,1)S(1)}, u32[]{:S(2)}, u32[]{:S(2)}) async-start(bf16[16,32,512]{2,1,0:T(8,128)(2,1)} %get-tuple-element.55), calls=%async_computation.1 | async-start | bytes 1048576 | tf_op jit(solution)/shard_map/all_to_all | solution.py:810
  22.0 13.9 %forward.1 = (bf16[16,512]{1,0:T(8,128)(2,1)S(1)}, f32[448,512]{1,0:T(8,128)S(1)}, bf16[448,512]{1,0:T(8,128)(2,1)S(1)}, bf16[512,512]{1,0:T(8,128)(2,1)S(1)}, b...) custom-call(f32[32,1,128]{2,1,0:T(1,128)S(1)} %all-to-all-done.refs_, ...), custom_call_target="tpu_custom_call" | custom-call | tf_op jit(solution)/shard_map/forward/pallas_call | solution.py:653
  35.9 0.5 all-to-all-done.1.refs_7_
  36.4 28.3 %backward.1 = (bf16[1024,512]{1,0:T(8,128)(2,1)}, f32[27,512]{1,0:T(8,128)}, f32[2,512]{1,0:T(2,128)}, f32[2,512]{1,0:T(2,128)}, f32[2,512]{1,0:T(2,128)}, /*ind...) custom-call(s32[1]{0:T(128)} %bitcast.refs_0_, ...), custom_call_target="tpu_custom_call" | custom-call | tf_op jit(solution)/shard_map/backward/pallas_call | solution.py:653
Async XLA Ops:
  3.4 7.9 %collective-permute-start = (f32[32,512]{1,0:T(8,128)S(1)}, f32[32,512]{1,0:T(8,128)S(1)}, u32[]{:S(2)}, u32[]{:S(2)}) collective-permute-start(f32[32,512]{1,0:T(8,128)S(1)} %get-tuple-element.49.refs_0_), channel_id=1, source_target_pairs={{0,1},{1,0},{2,3},{3,2},{4,5},{5,4},{6,7},{7,6},{8,9},{9,8},{10,11... | collective-permute-start | bytes 196616 | tf_op jit(solution)/shard_map/ppermute | solution.py:793
  6.3 12.1 %all-to-all-start = ((f32[32,1,128]{2,1,0:T(1,128)}), f32[32,1,128]{2,1,0:T(1,128)S(1)}, u32[]{:S(2)}, u32[]{:S(2)}) async-start(f32[32,1,128]{2,1,0:T(1,128)} %get-tuple-element.48), calls=%async_computation | async-start | bytes 32768 | tf_op jit(solution)/shard_map/all_to_all | solution.py:791
  18.4 18.0 %all-to-all-start.1 = ((bf16[16,32,512]{2,1,0:T(8,128)(2,1)}), bf16[16,32,512]{2,1,0:T(8,128)(2,1)S(1)}, u32[]{:S(2)}, u32[]{:S(2)}) async-start(bf16[16,32,512]{2,1,0:T(8,128)(2,1)} %get-tuple-element.55), calls=%async_computation.1 | async-start | bytes 1048576 | tf_op jit(solution)/shard_map/all_to_all | solution.py:810
